TPU v7x, 256 devices: a whole 4x4x8 slice. The times are simulated.
256 devices in a mesh: grp: 8 (over x, core), shard: 32 (over y, z).
Axes of the slice: x: 4, y: 4, z: 8, core: 2. Of those that a mesh axis runs over, the one named last changes fastest.
Arguments:
- features: bfloat16 [262144, 1280], P(('grp', 'shard')), parts along dimension 0
- norm_gain: float32 [1280], replicated, may hold values from 0.1 to 1.9
- norm_shift: float32 [1280], replicated, may hold values from -3 to 3
- merge_weight: bfloat16 [2560, 1280], P('shard'), may hold values from -0.125 to 0.125
- out_weight: bfloat16 [1280, 1280], P('shard'), may hold values from -0.15625 to 0.15625
- corr_src: int32 [2048, 3], P('grp'), parts along dimension 0, may hold values from 0 to 255, as said below
- corr_count: int32 [2048], P('grp'), parts along dimension 0, may hold values from 1 to 3
Outputs:
- block_out: bfloat16 [262144, 1280], P(('grp', 'shard')), parts along dimension 0
There are 8 independent parts, one for each index of `grp`. A program takes and returns all parts, laid end to end along the dimension named above; an argument that names none is the same for every part. Nothing has to cross between parts.
Inputs may be any that keep to these rules, and one draw needn't show every extreme that they name: `corr_src`: every source block belongs to another view than the block that lists it. Over all 24 slots of one view's blocks (valid or not), the source blocks of any one other view number at most 1, and that number is reached.
All inputs are finite; a program needn't handle non-finite values.
Results may differ from a plain program's by a relative error of at most 0.0018.
Values may be sent and summed in bfloat16 or wider, within the bound.
A program may use at most 128 MiB of HBM per device.

v0:
```python
import jax
import jax.numpy as jnp
from jax import lax
from jax.sharding import PartitionSpec as P

GROUPS = 32
BLOCK = 128


def per_device(features, norm_gain, norm_shift, merge_weight, out_weight, corr_src, corr_count):
    devices = lax.axis_size("shard")
    device = lax.axis_index("shard")
    rows_here, channels = features.shape
    blocks = rows_here // BLOCK
    slot_count = corr_src.shape[1]
    group_width = channels // GROUPS
    members = float(rows_here * group_width)

    def group_norm(values):
        grouped = values.reshape(rows_here, GROUPS, group_width)
        average = jnp.sum(grouped, axis=(0, 2), keepdims=True) / members
        centered = grouped - average
        variance = jnp.sum(centered * centered, axis=(0, 2), keepdims=True) / members
        return (centered * lax.rsqrt(variance + 1e-05)).reshape(rows_here, channels)

    inputs = features.astype(jnp.float32)
    hidden = jax.nn.silu(group_norm(inputs) * norm_gain + norm_shift).astype(jnp.bfloat16)
    hidden_blocks = hidden.reshape(blocks, BLOCK, channels)
    entries = blocks * slot_count
    capacity = (entries + devices - 2) // (devices - 1)
    order = jnp.arange(entries, dtype=jnp.int32)
    own_list = lax.dynamic_slice_in_dim(corr_src, device * blocks, blocks, 0).reshape(entries)
    sender = own_list // blocks
    local_block = own_list % blocks
    earlier = (sender[:, None] == sender[None, :]) & (order[None, :] < order[:, None])
    ranking = jnp.sum(earlier.astype(jnp.int32), axis=1)
    place = sender * capacity + ranking
    matches = place[:, None] == jnp.arange(devices * capacity, dtype=jnp.int32)[None, :]
    requests = jnp.sum(jnp.where(matches, local_block[:, None], 0), axis=0).reshape(
        devices, capacity
    )
    arrived = lax.all_to_all(
        jnp.take(
            hidden_blocks,
            lax.all_to_all(requests, "shard", split_axis=0, concat_axis=0, tiled=True),
            axis=0,
        ),
        "shard",
        split_axis=0,
        concat_axis=0,
        tiled=True,
    )
    pooled = jnp.take(arrived.reshape(devices * capacity, BLOCK, channels), place, axis=0)
    pooled = pooled.reshape(blocks, slot_count, BLOCK, channels)
    counts = lax.dynamic_slice_in_dim(corr_count, device * blocks, blocks, 0)
    valid = (jnp.arange(slot_count, dtype=jnp.int32)[None, :] < counts[:, None]).astype(jnp.float32)
    summed = jnp.zeros((blocks, BLOCK, channels), jnp.float32)
    for position in range(slot_count):
        summed = summed + pooled[:, position].astype(jnp.float32) * valid[:, position, None, None]
    divisor = counts.astype(jnp.float32)[:, None, None]
    epipolar = (summed / divisor).astype(jnp.bfloat16).reshape(rows_here, channels)
    joined = jnp.concatenate([hidden, epipolar], axis=1)
    columns = joined
    merged = jnp.dot(
        columns,
        lax.all_gather(merge_weight, "shard", axis=0, tiled=True),
        preferred_element_type=jnp.float32,
    )
    activated = jax.nn.silu(group_norm(merged)).astype(jnp.bfloat16)
    columns = activated
    projected = jnp.dot(
        columns,
        lax.all_gather(out_weight, "shard", axis=0, tiled=True),
        preferred_element_type=jnp.float32,
    )
    return (inputs + projected).astype(jnp.bfloat16)


def solution(mesh):
    placed = (
        P(("grp", "shard"), None),
        P(),
        P(),
        P("shard", None),
        P("shard", None),
        P("grp", None),
        P("grp"),
    )
    return jax.shard_map(
        per_device, mesh=mesh, in_specs=placed, out_specs=P(("grp", "shard"), None), check_vma=False
    )
```

profile of v0, /device:TPU:1, one launch (start us, length us, event | category | flops | bytes accessed | tf_op | source)
XLA Modules:
  0.0 384.8 jit_solution(13887879820677833971)
XLA Ops:
  6.5 0.7 copy-done
  7.5 0.2 convert_reduce_fusion.1
  7.7 0.1 select_reduce_fusion
  7.8 0.7 copy.16
  8.5 12.0 %all-to-all-start = ((s32[32,1,1]{2,1,0:T(1,128)}), s32[32,1,1]{2,1,0:T(1,128)S(1)}, u32[]{:S(2)}, u32[]{:S(2)}) async-start(s32[32,1,1]{2,1,0:T(1,128)} %copy.16), calls=%async_computation | async-start | bytes 32768 | tf_op jit(solution)/shard_map/all_to_all | solution.py:45
  20.5 2.2 convert_reduce_fusion
  22.8 0.1 reduce_sum.69
  23.0 0.1 sub.37
  23.0 2.5 fusion.2
  25.6 0.1 reduce_sum.75
  25.8 0.1 mul.100
  25.9 3.5 fusion.10
  29.5 0.7 and_reduce_fusion
  30.2 0.7 reduce.9
  30.8 5.8 %gather_fusion = bf16[32,128,1280]{2,1,0:T(8,128)(2,1)} fusion(bf16[8,128,1280]{2,1,0:T(8,128)(2,1)S(1)} %bitcast.37, s32[1024]{0:T(1024)S(1)} %pad_clamp_fusion.1), kind=kCustom, calls=%fused_computation | custom fusion | bytes 20971648 | tf_op jit(solution)/shard_map/jit(_take)/gather | solution.py:43
  36.6 10.1 %bitcast_select_fusion = bf16[32,1,128,1280]{3,2,1,0:T(8,128)(2,1)} fusion(bf16[32,128,1280]{2,1,0:T(8,128)(2,1)} %gather_fusion, pred[32]{0:T(512)(128)(4,1)S(1)} %get-tuple-element.7), kind=kLoop, calls=%fused_computation.2 | loop fusion | flops 5242880 | bytes 20971552 | tf_op jit(solution)/shard_map/jit(_take)/select_n | solution.py:43
  46.8 9.5 %all-to-all-start.1 = ((bf16[32,1,128,1280]{3,2,1,0:T(8,128)(2,1)}), bf16[32,1,128,1280]{3,2,1,0:T(8,128)(2,1)}, u32[]{:S(2)}, u32[]{:S(2)}) async-start(bf16[32,1,128,1280]{3,2,1,0:T(8,128)(2,1)} %bitcast_select_fusion), calls=%async_computation.1 | async-start | bytes 20971520 | tf_op jit(solution)/shard_map/all_to_all | solution.py:42
  56.3 0.7 all-gather.3.cloned.1.call-update
  57.0 0.2 all-gather.5.cloned.1.call-start
  57.2 0.5 all-gather.5.cloned.1.call-update
  58.2 270.9 %all-to-all-done.1 = bf16[32,1,128,1280]{3,2,1,0:T(8,128)(2,1)} async-done(((bf16[32,1,128,1280]{3,2,1,0:T(8,128)(2,1)}), bf16[32,1,128,1280]{3,2,1,0:T(8,128)(2,1)}, u32[]{:S(2)}, u32[]{:S(2)}) %all-to-all-start.1) | async-done | bytes 10485792 | tf_op jit(solution)/shard_map/all_to_all | solution.py:42
  329.0 9.2 %gather_fusion.1 = bf16[24,128,1280]{2,1,0:T(8,128)(2,1)} fusion(bf16[32,128,1280]{2,1,0:T(8,128)(2,1)} %bitcast.3, s32[1024]{0:T(1024)S(1)} %pad_clamp_fusion), kind=kCustom, calls=%fused_computation.1 | custom fusion | bytes 15728736 | tf_op jit(solution)/shard_map/jit(_take)/gather | solution.py:53
  338.2 7.1 %broadcast_select_fusion = bf16[8,3,128,1280]{3,2,1,0:T(8,128)(2,1)} fusion(bf16[8,3,128,1280]{3,2,1,0:T(8,128)(2,1)} %bitcast.38, pred[8,3]{1,0:T(8,128)(4,1)S(1)} %compare_and_fusion), kind=kLoop, calls=%fused_computation.6 | loop fusion | flops 3932160 | bytes 15728664 | tf_op jit(solution)/shard_map/jit(_take)/select_n | solution.py:53
  345.4 3.7 fusion.31
  349.1 3.4 fusion.18
  352.5 12.0 %fusion.32 = (f32[1280]{0:T(1024)S(1)}, f32[1024,1280]{1,0:T(8,128)}) fusion(bf16[2560,1280]{1,0:T(8,128)(2,1)} %all-gather.3.cloned.1.call-done, bf16[1024,1280]{1,0:T(8,128)(2,1)} %fusion.18, bf16[1024,1280]{1,0:T(8,128)(2,1)S(1)} %fusion.10), kind=kOutput, calls=%fused_computation.83 | convolution fusion | flops 6722681856 | bytes 17044480 | tf_op jit(solution)/shard_map/dot_general | solution.py:64
  364.6 0.1 reduce_sum.98
  364.8 0.1 sub.44
  364.9 3.3 multiply_reduce_fusion
  368.2 0.1 reduce_sum.101
  368.4 0.1 mul.124
  368.6 9.4 %fusion.11 = bf16[1024,1280]{1,0:T(8,128)(2,1)} fusion(bf16[1024,1280]{1,0:T(8,128)(2,1)S(1)} %copy-done.2, bf16[1280,1280]{1,0:T(8,128)(2,1)} %all-gather.5.cloned.1.call-done, f32[1024,1280]{1,0:T(8,128)} %get-tuple-element.18, f32[1280]{0:T(1024)S(1)} %mul.124, f32[1280]{0:T(1024)S(1)} %sub.44), kind=kOutput, calls=%fused_computation.18 | convolution fusion | flops 3368550400 | bytes 13772800 | tf_op jit(solution)/shard_map/dot_general | solution.py:71
  (43 shorter events, 1.4 us)
Async XLA Ops:
  6.5 0.7 copy-start
  6.5 19.4 %copy-start.4 = (f32[1280]{0:T(1024)S(1)}, f32[1280]{0:T(1024)}, u32[]{:S(2)}) copy-start(f32[1280]{0:T(1024)} %param.8) | copy-start | bytes 15364
  6.5 19.4 %copy-start.3 = (f32[1280]{0:T(1024)S(1)}, f32[1280]{0:T(1024)}, u32[]{:S(2)}) copy-start(f32[1280]{0:T(1024)} %param.9) | copy-start | bytes 15364
  8.5 21.0 %all-to-all-start = ((s32[32,1,1]{2,1,0:T(1,128)}), s32[32,1,1]{2,1,0:T(1,128)S(1)}, u32[]{:S(2)}, u32[]{:S(2)}) async-start(s32[32,1,1]{2,1,0:T(1,128)} %copy.16), calls=%async_computation | async-start | bytes 32768 | tf_op jit(solution)/shard_map/all_to_all | solution.py:45
  46.8 11.1 %copy-start.5 = (s32[256]{0:T(256)S(1)}, s32[256]{0:T(256)}, u32[]{:S(2)}) copy-start(s32[256]{0:T(256)} %param.13) | copy-start | bytes 3076
  46.8 282.3 %all-to-all-start.1 = ((bf16[32,1,128,1280]{3,2,1,0:T(8,128)(2,1)}), bf16[32,1,128,1280]{3,2,1,0:T(8,128)(2,1)}, u32[]{:S(2)}, u32[]{:S(2)}) async-start(bf16[32,1,128,1280]{3,2,1,0:T(8,128)(2,1)} %bitcast_select_fusion), calls=%async_computation.1 | async-start | bytes 20971520 | tf_op jit(solution)/shard_map/all_to_all | solution.py:42
  56.2 296.3 %all-gather.3.cloned.1.call-start = ((), (), s32[]{:S(2)}) async-start(), calls=%async_computation.2 | async-start | bytes 6758400 | tf_op jit(solution)/shard_map/all_gather | solution.py:66
  57.0 311.6 %all-gather.5.cloned.1.call-start = ((), (), s32[]{:S(2)}) async-start(), calls=%async_computation.3 | async-start | bytes 3379200 | tf_op jit(solution)/shard_map/all_gather | solution.py:73
  364.5 4.1 %copy-start.2 = (bf16[1024,1280]{1,0:T(8,128)(2,1)S(1)}, bf16[1024,1280]{1,0:T(8,128)(2,1)}, u32[]{:S(2)}) copy-start(bf16[1024,1280]{1,0:T(8,128)(2,1)} %param.7) | copy-start | bytes 7864324
  368.6 9.4 %copy-start.1 = (s32[256,3]{0,1:T(4,128)S(1)}, s32[256,3]{0,1:T(4,128)}, u32[]{:S(2)}) copy-start(s32[256,3]{0,1:T(4,128)} %param.12) | copy-start | bytes 9220
Sparse Core Ops, SparseCore 0:
  59.7 186.5 all-gather.2
  248.9 115.3 all-gather.4
where the time goes:
time: 387 us; the launch traced here: 385 us
  waiting for transfers between devices  272 us (70%)
  other arithmetic  34.3 us (9%)
  starting transfers between devices  21.8 us (6%)
  local copies, waits for them, and re-layouts  21.6 us (6%)
  matrix products  21.4 us (6%)
  between operations  13.6 us (4%)
    all_to_all x1, waiting for transfers between devices, per_device(): lax.all_to_all(jnp.take(hidden_blocks, lax.all_to_all(requests, 'shard',...  271 us
    all_to_all x1, starting transfers between devices, per_device(): lax.all_to_all(requests, 'shard', split_axis=0, concat_axis=0, tiled=True)  12 us
    dot_general x1, matrix products, per_device(): jnp.dot(columns, lax.all_gather(merge_weight, 'shard', axis=0, tiled=True...  12 us
    select_n x2, other arithmetic, per_device(): jnp.take(hidden_blocks, lax.all_to_all(requests, 'shard', split_axis=0, c...  10.8 us
    all_to_all x1, starting transfers between devices, per_device(): lax.all_to_all(jnp.take(hidden_blocks, lax.all_to_all(requests, 'shard',...  9.47 us
    dot_general x1, matrix products, per_device(): jnp.dot(columns, lax.all_gather(out_weight, 'shard', axis=0, tiled=True),...  9.35 us
    gather x1, local copies, waits for them, and re-layouts, per_device(): jnp.take(arrived.reshape(devices * capacity, BLOCK, channels), place, axi...  9.19 us
  transfers between devices with their start and end apart: 4, of which 1 were waited for; matrix products, arithmetic and copies ran while one was open for 13% of the time, Pallas kernels for 0%

commit v1 on v0

v1 whole, which is shorter than its diff:
```python
import jax
import jax.numpy as jnp
from jax import lax
from jax.sharding import PartitionSpec as P

GROUPS = 32
BLOCK = 128


def per_device(features, norm_gain, norm_shift, merge_weight, out_weight, corr_src, corr_count):
    devices = lax.axis_size("shard")
    rows_here, channels = features.shape
    blocks = rows_here // BLOCK
    slot_count = corr_src.shape[1]
    group_width = channels // GROUPS
    members = float(rows_here * group_width)
    slice_rows = BLOCK // devices
    all_blocks = corr_src.shape[0]

    def group_norm(values):
        grouped = values.reshape(rows_here, GROUPS, group_width)
        average = jnp.sum(grouped, axis=(0, 2), keepdims=True) / members
        centered = grouped - average
        variance = jnp.sum(centered * centered, axis=(0, 2), keepdims=True) / members
        return (centered * lax.rsqrt(variance + 1e-05)).reshape(rows_here, channels)

    inputs = features.astype(jnp.float32)
    hidden = jax.nn.silu(group_norm(inputs) * norm_gain + norm_shift).astype(jnp.bfloat16)
    slices = hidden.reshape(blocks, devices, slice_rows, channels).transpose(1, 0, 2, 3)
    arrived = lax.all_to_all(slices, "shard", split_axis=0, concat_axis=0, tiled=True)
    arrived = arrived.reshape(all_blocks, slice_rows, channels)
    valid = (jnp.arange(slot_count, dtype=jnp.int32)[None, :] < corr_count[:, None]).astype(jnp.float32)
    summed = jnp.zeros((all_blocks, slice_rows, channels), jnp.float32)
    for position in range(slot_count):
        picked = jnp.take(arrived, corr_src[:, position], axis=0, mode="clip")
        summed = summed + picked.astype(jnp.float32) * valid[:, position, None, None]
    divisor = corr_count.astype(jnp.float32)[:, None, None]
    pooled = (summed / divisor).astype(jnp.bfloat16).reshape(devices, blocks, slice_rows, channels)
    back = lax.all_to_all(pooled, "shard", split_axis=0, concat_axis=0, tiled=True)
    epipolar = back.transpose(1, 0, 2, 3).reshape(rows_here, channels)
    joined = jnp.concatenate([hidden, epipolar], axis=1)
    merged = jnp.dot(
        joined,
        lax.all_gather(merge_weight, "shard", axis=0, tiled=True),
        preferred_element_type=jnp.float32,
    )
    activated = jax.nn.silu(group_norm(merged)).astype(jnp.bfloat16)
    projected = jnp.dot(
        activated,
        lax.all_gather(out_weight, "shard", axis=0, tiled=True),
        preferred_element_type=jnp.float32,
    )
    return (inputs + projected).astype(jnp.bfloat16)


def solution(mesh):
    placed = (
        P(("grp", "shard"), None),
        P(),
        P(),
        P("shard", None),
        P("shard", None),
        P("grp", None),
        P("grp"),
    )
    return jax.shard_map(
        per_device, mesh=mesh, in_specs=placed, out_specs=P(("grp", "shard"), None), check_vma=False
    )
```

time: 387 us -> 253 us (0.65)
  waiting for transfers between devices: 272 us -> 138 us
  other arithmetic: 34.3 us -> 16.3 us
  local copies, waits for them, and re-layouts: 21.6 us -> 37.5 us
    all_to_all x2, waiting for transfers between devices: 271 us -> 137 us  [the longest x1 74 us: per_device(): lax.all_to_all(slices, 'shard', split_axis=0, concat_axis=0, tiled=True)]
    select_n x5 -> x0, other arithmetic: 17.9 us -> none  [the longest x2 10.8 us: per_device(): jnp.take(hidden_blocks, lax.all_to_all(requests, 'shard', split_axis=0, c...]
    reshape x2 -> x4, local copies, waits for them, and re-layouts: 0.16 us -> 15.4 us  [the longest x2 8.05 us: per_device(): hidden.reshape(blocks, devices, slice_rows, channels).transpose(1, 0, 2, 3)]
    transpose x0 -> x1, local copies, waits for them, and re-layouts: none -> 4.48 us  [per_device(): epipolar = back.transpose(1, 0, 2, 3).reshape(rows_here, channels)]
    gather x2 -> x3, local copies, waits for them, and re-layouts: 15 us -> 12.7 us  [per_device(): picked = jnp.take(arrived, corr_src[:, position], axis=0, mode='clip')]
  transfers between devices with their start and end apart: 4 -> 4, of which waited for: 1 -> 2; matrix products, arithmetic and copies ran while one was open for 13% -> 26% of each run, Pallas kernels for 0% -> 0%
where the time goes in v1:
time: 253 us; the launch traced here: 249 us
  waiting for transfers between devices  138 us (55%)
  local copies, waits for them, and re-layouts  37.5 us (15%)
  starting transfers between devices  22.5 us (9%)
  matrix products  21.3 us (8%)
  other arithmetic  16.3 us (6%)
  between operations  13.6 us (5%)
    all_to_all x1, waiting for transfers between devices, per_device(): lax.all_to_all(slices, 'shard', split_axis=0, concat_axis=0, tiled=True)  74 us
    all_to_all x1, waiting for transfers between devices, per_device(): lax.all_to_all(pooled, 'shard', split_axis=0, concat_axis=0, tiled=True)  62.9 us
    gather x3, local copies, waits for them, and re-layouts, per_device(): picked = jnp.take(arrived, corr_src[:, position], axis=0, mode='clip')  12.7 us
    all_to_all x1, starting transfers between devices, per_device(): lax.all_to_all(slices, 'shard', split_axis=0, concat_axis=0, tiled=True)  12.2 us
    dot_general x1, matrix products, per_device(): jnp.dot(joined, lax.all_gather(merge_weight, 'shard', axis=0, tiled=True)...  12 us
    all_to_all x1, starting transfers between devices, per_device(): lax.all_to_all(pooled, 'shard', split_axis=0, concat_axis=0, tiled=True)  9.97 us
    dot_general x1, matrix products, per_device(): jnp.dot(activated, lax.all_gather(out_weight, 'shard', axis=0, tiled=True...  9.33 us
    reshape x2, local copies, waits for them, and re-layouts, per_device(): hidden.reshape(blocks, devices, slice_rows, channels).transpose(1, 0, 2, 3)  8.05 us
  transfers between devices with their start and end apart: 4, of which 2 were waited for; matrix products, arithmetic and copies ran while one was open for 26% of the time, Pallas kernels for 0%

profile of v1, /device:TPU:1, one launch (start us, length us, event | category | flops | bytes accessed | tf_op | source)
XLA Modules:
  0.0 249.2 jit_solution(9185796561827240515)
XLA Ops:
  6.5 0.7 all-gather.3.cloned.1.call-update
  7.3 2.3 convert_reduce_fusion
  9.6 0.1 reduce_sum.51
  9.8 0.1 sub.29
  9.9 2.5 fusion.2
  12.5 0.1 reduce_sum.54
  12.7 0.1 mul.84
  12.8 3.3 %fusion.10 = bf16[1024,1280]{1,0:T(8,128)(2,1)} fusion(bf16[1024,1280]{1,0:T(8,128)(2,1)S(1)} %copy-done, f32[1280]{0:T(1024)S(1)} %copy-done.4, f32[1280]{0:T(1024)S(1)} %copy-done.5, f32[1280]{0:T(1024)S(1)} %mul.84, f32[1280]{0:T(1024)S(1)} %sub.29), kind=kLoop, calls=%fused_computation.16 | loop fusion | flops 13107200 | bytes 5263360 | tf_op jit(solution)/shard_map/convert_element_type | solution.py:28
  16.1 4.3 %reshape.72 = bf16[8,32,4,1280]{3,2,1,0:T(4,128)(2,1)S(1)} reshape(bf16[1024,1280]{1,0:T(8,128)(2,1)} %fusion.10) | data formatting | bytes 5242880 | tf_op jit(solution)/shard_map/reshape | solution.py:29
  20.4 3.7 %copy.54 = bf16[8,32,4,1280]{3,0,2,1:T(8,128)(2,1)} copy(bf16[8,32,4,1280]{3,2,1,0:T(4,128)(2,1)S(1)} %reshape.72) | data formatting | bytes 5242880 | tf_op jit(solution)/shard_map/reshape | solution.py:29
  24.2 12.2 %all-to-all-start = ((bf16[32,8,4,1280]{3,1,2,0:T(8,128)(2,1)}), bf16[32,8,4,1280]{3,1,2,0:T(8,128)(2,1)S(1)}, u32[]{:S(2)}, u32[]{:S(2)}) async-start(bf16[32,8,4,1280]{3,1,2,0:T(8,128)(2,1)} %bitcast.21), calls=%async_computation | async-start | bytes 5242880 | tf_op jit(solution)/shard_map/all_to_all | solution.py:30
  36.9 74.0 %all-to-all-done = bf16[32,8,4,1280]{3,1,2,0:T(8,128)(2,1)S(1)} async-done(((bf16[32,8,4,1280]{3,1,2,0:T(8,128)(2,1)}), bf16[32,8,4,1280]{3,1,2,0:T(8,128)(2,1)S(1)}, u32[]{:S(2)}, u32[]{:S(2)}) %all-to-all-start) | async-done | bytes 2621472 | tf_op jit(solution)/shard_map/all_to_all | solution.py:30
  110.9 0.2 copy.53
  111.0 2.0 copy.40
  113.1 4.3 %gather_fusion = bf16[256,4,1280]{2,1,0:T(4,128)(2,1)} fusion(bf16[256,4,1280]{2,1,0:T(4,128)(2,1)S(1)} %copy.40, s32[1024]{0:T(1024)S(1)} %pad_clamp_fusion.2), kind=kCustom, calls=%fused_computation | custom fusion | bytes 5243904 | tf_op jit(solution)/shard_map/jit(_take)/gather | solution.py:35
  117.4 4.2 %gather_fusion.1 = bf16[256,4,1280]{2,1,0:T(4,128)(2,1)} fusion(bf16[256,4,1280]{2,1,0:T(4,128)(2,1)S(1)} %copy.40, s32[1024]{0:T(1024)S(1)} %pad_clamp_fusion.1), kind=kCustom, calls=%fused_computation.1 | custom fusion | bytes 5243904 | tf_op jit(solution)/shard_map/jit(_take)/gather | solution.py:35
  121.5 4.3 %gather_fusion.2 = bf16[256,4,1280]{2,1,0:T(4,128)(2,1)} fusion(bf16[256,4,1280]{2,1,0:T(4,128)(2,1)S(1)} %copy.40, s32[1024]{0:T(1024)S(1)} %pad_clamp_fusion), kind=kCustom, calls=%fused_computation.2 | custom fusion | bytes 5243904 | tf_op jit(solution)/shard_map/jit(_take)/gather | solution.py:35
  125.8 4.5 %fusion.18 = bf16[32,8,4,1280]{3,1,0,2:T(8,128)(2,1)S(1)} fusion(bf16[256,4,1280]{2,1,0:T(4,128)(2,1)} %gather_fusion.2, bf16[256,4,1280]{2,1,0:T(4,128)(2,1)} %gather_fusion.1, bf16[256,4,1280]{2,1,0:T(4,128)(2,1)} %gather_fusion, f32[32,8]{1,0:T(8,128)S(1)} %div.33, f32[32,8]{1,0:T(8,128)S(1)} %mul.96, f32[32,8]{1,0:T(8,128)S(1)} %mul.93, f32[32,8]{1,0:T(8,128)S(1)} %mul.90), kind=kLoop, calls=%fused_computation.25 | loop fusion | flops 13107200 | bytes 10489856 | tf_op jit(solution)/shard_map/convert_element_type | solution.py:38
  130.3 1.9 copy.46
  132.2 10.0 %all-to-all-start.1 = ((bf16[32,8,4,1280]{3,1,2,0:T(8,128)(2,1)}), bf16[32,8,4,1280]{3,1,2,0:T(8,128)(2,1)S(1)}, u32[]{:S(2)}, u32[]{:S(2)}) async-start(bf16[32,8,4,1280]{3,1,2,0:T(8,128)(2,1)} %copy.46), calls=%async_computation.1 | async-start | bytes 5242880 | tf_op jit(solution)/shard_map/all_to_all | solution.py:39
  142.2 0.3 all-gather.5.cloned.1.call-start
  142.4 0.5 all-gather.5.cloned.1.call-update
  142.9 62.9 %all-to-all-done.1 = bf16[32,8,4,1280]{3,1,2,0:T(8,128)(2,1)S(1)} async-done(((bf16[32,8,4,1280]{3,1,2,0:T(8,128)(2,1)}), bf16[32,8,4,1280]{3,1,2,0:T(8,128)(2,1)S(1)}, u32[]{:S(2)}, u32[]{:S(2)}) %all-to-all-start.1) | async-done | bytes 2621472 | tf_op jit(solution)/shard_map/all_to_all | solution.py:39
  205.8 1.5 copy-done.3
  207.2 4.5 %copy.47 = bf16[8,32,4,1280]{3,2,1,0:T(4,128)(2,1)} copy(bf16[8,32,4,1280]{3,0,2,1:T(8,128)(2,1)} %bitcast.22) | data formatting | bytes 5242880 | tf_op jit(solution)/shard_map/transpose | solution.py:40
  211.7 5.3 %reshape.74 = bf16[1024,1280]{1,0:T(8,128)(2,1)} reshape(bf16[8,32,4,1280]{3,2,1,0:T(4,128)(2,1)} %copy.47) | data formatting | bytes 5242880 | tf_op jit(solution)/shard_map/reshape | solution.py:40
  217.0 12.0 %fusion.26 = (f32[1280]{0:T(1024)S(1)}, f32[1024,1280]{1,0:T(8,128)}) fusion(bf16[2560,1280]{1,0:T(8,128)(2,1)} %all-gather.3.cloned.1.call-done, bf16[1024,1280]{1,0:T(8,128)(2,1)} %reshape.74, bf16[1024,1280]{1,0:T(8,128)(2,1)S(1)} %copy-done.2), kind=kOutput, calls=%fused_computation.50 | convolution fusion | flops 6722681856 | bytes 17044480 | tf_op jit(solution)/shard_map/dot_general | solution.py:42
  229.1 0.1 reduce_sum.72
  229.4 3.3 %multiply_reduce_fusion = f32[1280]{0:T(1024)S(1)} fusion(f32[1024,1280]{1,0:T(8,128)} %get-tuple-element.12, f32[1280]{0:T(1024)S(1)} %sub.33), kind=kLoop, calls=%fused_computation.30 | loop fusion | flops 3930880 | bytes 5253120 | tf_op jit(solution)/shard_map/reduce_sum | solution.py:24
  232.7 0.1 reduce_sum.75
  232.9 0.1 mul.101
  233.1 9.3 %fusion.11 = bf16[1024,1280]{1,0:T(8,128)(2,1)} fusion(bf16[1024,1280]{1,0:T(8,128)(2,1)S(1)} %copy-done.1, bf16[1280,1280]{1,0:T(8,128)(2,1)} %all-gather.5.cloned.1.call-done, f32[1024,1280]{1,0:T(8,128)} %get-tuple-element.12, f32[1280]{0:T(1024)S(1)} %mul.101, f32[1280]{0:T(1024)S(1)} %sub.33), kind=kOutput, calls=%fused_computation.17 | convolution fusion | flops 3368550400 | bytes 13772800 | tf_op jit(solution)/shard_map/dot_general | solution.py:48
  (42 shorter events, 1.2 us)
Async XLA Ops:
  6.5 6.2 %copy-start = (bf16[1024,1280]{1,0:T(8,128)(2,1)S(1)}, bf16[1024,1280]{1,0:T(8,128)(2,1)}, u32[]{:S(2)}) copy-start(bf16[1024,1280]{1,0:T(8,128)(2,1)} %param.7) | copy-start | bytes 7864324
  6.5 6.2 %copy-start.5 = (f32[1280]{0:T(1024)S(1)}, f32[1280]{0:T(1024)}, u32[]{:S(2)}) copy-start(f32[1280]{0:T(1024)} %param.8) | copy-start | bytes 15364
  6.5 6.2 %copy-start.4 = (f32[1280]{0:T(1024)S(1)}, f32[1280]{0:T(1024)}, u32[]{:S(2)}) copy-start(f32[1280]{0:T(1024)} %param.9) | copy-start | bytes 15364
  6.5 210.5 %all-gather.3.cloned.1.call-start = ((), (), s32[]{:S(2)}) async-start(), calls=%async_computation.2 | async-start | bytes 6758400 | tf_op jit(solution)/shard_map/all_gather | solution.py:44
  20.4 16.0 %copy-start.6 = (s32[256]{0:T(256)S(1)}, s32[256]{0:T(256)}, u32[]{:S(2)}) copy-start(s32[256]{0:T(256)} %param.13) | copy-start | bytes 3076
  20.4 16.4 %copy-start.7 = (s32[256,3]{0,1:T(4,128)S(1)}, s32[256,3]{0,1:T(4,128)}, u32[]{:S(2)}) copy-start(s32[256,3]{0,1:T(4,128)} %param.12) | copy-start | bytes 9220
  24.2 86.7 %all-to-all-start = ((bf16[32,8,4,1280]{3,1,2,0:T(8,128)(2,1)}), bf16[32,8,4,1280]{3,1,2,0:T(8,128)(2,1)S(1)}, u32[]{:S(2)}, u32[]{:S(2)}) async-start(bf16[32,8,4,1280]{3,1,2,0:T(8,128)(2,1)} %bitcast.21), calls=%async_computation | async-start | bytes 5242880 | tf_op jit(solution)/shard_map/all_to_all | solution.py:30
  132.2 73.6 %all-to-all-start.1 = ((bf16[32,8,4,1280]{3,1,2,0:T(8,128)(2,1)}), bf16[32,8,4,1280]{3,1,2,0:T(8,128)(2,1)S(1)}, u32[]{:S(2)}, u32[]{:S(2)}) async-start(bf16[32,8,4,1280]{3,1,2,0:T(8,128)(2,1)} %copy.46), calls=%async_computation.1 | async-start | bytes 5242880 | tf_op jit(solution)/shard_map/all_to_all | solution.py:39
  142.2 90.9 %all-gather.5.cloned.1.call-start = ((), (), s32[]{:S(2)}) async-start(), calls=%async_computation.3 | async-start | bytes 3379200 | tf_op jit(solution)/shard_map/all_gather | solution.py:50
  205.8 1.5 copy-start.3
  207.2 9.8 %copy-start.2 = (bf16[1024,1280]{1,0:T(8,128)(2,1)S(1)}, bf16[1024,1280]{1,0:T(8,128)(2,1)}, u32[]{:S(2)}) copy-start(bf16[1024,1280]{1,0:T(8,128)(2,1)} %fusion.10) | copy-start | bytes 7864324
  229.0 4.0 %copy-start.1 = (bf16[1024,1280]{1,0:T(8,128)(2,1)S(1)}, bf16[1024,1280]{1,0:T(8,128)(2,1)}, u32[]{:S(2)}) copy-start(bf16[1024,1280]{1,0:T(8,128)(2,1)} %param.7) | copy-start | bytes 7864324
Sparse Core Ops, SparseCore 0:
  9.9 122.3 all-gather.2
  145.6 83.9 all-gather.4

commit v2 on v1

v2 whole, which is shorter than its diff:
```python
import functools

import jax
import jax.numpy as jnp
from jax import lax
from jax.experimental import pallas as pl
from jax.experimental.pallas import tpu as pltpu
from jax.sharding import PartitionSpec as P

GROUPS = 32
BLOCK = 128
LANES = 128
ROWS = 8
PIECE = 16
MESH = pl.DeviceIdType.MESH
F32 = jnp.float32
BF16 = jnp.bfloat16


def zigzag(center, place):
    odd = place % 2
    return center + (1 - odd) * (place // 2) - odd * ((place + 1) // 2)


def split_rows(row):
    high = row.astype(BF16).astype(F32)
    rest = row - high
    middle = rest.astype(BF16).astype(F32)
    low = rest - middle
    fill = jnp.zeros((PIECE - 3, row.shape[1]), F32)
    return jnp.concatenate([high, middle, low, fill], axis=0).astype(BF16)


def group_mean(row, collect, spread, members):
    parts = jnp.dot(split_rows(row), collect[...], preferred_element_type=F32)
    mean = (parts[0:1] + parts[1:2] + parts[2:3]) / members
    parts = jnp.dot(split_rows(mean), spread[...], preferred_element_type=F32)
    return parts[0:1] + parts[1:2] + parts[2:3]


def fold_rows(values):
    return jnp.sum(values.reshape(values.shape[0] // ROWS, ROWS, values.shape[1]), axis=0)


def silu(values):
    return values / (1.0 + jnp.exp(-values))


def kernel(
    sizes,
    x_hbm, gain_ref, shift_ref, merge_ref, outw_ref, src_ref, count_ref,
    out_hbm,
    x, stage, send1, recv1, send2, recv2, table, full, merge_w, out_w, acc, collect, spread, stats,
    load_sem, out_sem, pack_sem, s1_sem, r1_sem, s2_sem, r2_sem, ws_sem, wr_sem,
):
    ys, zs, xs, cores = sizes
    shards = ys * zs
    rows, channels = x.shape
    blocks = rows // BLOCK
    strips = BLOCK // ROWS
    halves = shards // strips
    half = channels // halves
    chunks = half // LANES
    pieces = full.shape[1]
    merge_rows = merge_ref.shape[0]
    out_rows = outw_ref.shape[0]
    merge_pieces = merge_rows // PIECE
    group_width = channels // GROUPS
    members = float(rows * group_width)
    slice_rows = blocks * ROWS

    s = lax.axis_index("shard")
    g = lax.axis_index("grp")
    y, z = s // zs, s % zs
    xx, core = g // cores, g % cores

    load = pltpu.make_async_copy(x_hbm, x, load_sem)
    load.start()

    def peer_of(step):
        dz = zigzag(zs // 2, step // ys)
        dy = zigzag(ys // 2, step % ys)
        return ((y + dy) % ys) * zs + (z + dz) % zs

    barrier = pltpu.get_barrier_semaphore()

    @pl.loop(0, shards - 1)
    def _(step):
        pl.semaphore_signal(barrier, inc=1, device_id=(g, peer_of(step)), device_id_type=MESH)

    for dx in range(1, xs):
        to = ((xx + dx) % xs) * cores + core
        pl.semaphore_signal(barrier, inc=1, device_id=(to, s), device_id_type=MESH)
    sibling = xx * cores + (core + 1) % cores
    pl.semaphore_signal(barrier, inc=1, device_id=(sibling, s), device_id_type=MESH)

    for piece in range(merge_pieces):
        stage[piece] = merge_ref[piece * PIECE : (piece + 1) * PIECE, :]
    whole = out_rows // PIECE
    for piece in range(whole):
        stage[merge_pieces + piece] = outw_ref[piece * PIECE : (piece + 1) * PIECE, :]
    rest = out_rows - whole * PIECE
    tail = outw_ref[whole * PIECE : out_rows, :].astype(F32)
    stage[merge_pieces + whole] = jnp.concatenate(
        [tail, jnp.zeros((PIECE - rest, channels), F32)], axis=0
    ).astype(BF16)

    lane = lax.broadcasted_iota(jnp.int32, (channels, LANES), 1) * group_width
    row = lax.broadcasted_iota(jnp.int32, (channels, LANES), 0)
    collect[...] = jnp.where((row >= lane) & (row < lane + group_width), 1.0, 0.0).astype(BF16)
    lane = lax.broadcasted_iota(jnp.int32, (LANES, channels), 1)
    row = lax.broadcasted_iota(jnp.int32, (LANES, channels), 0) * group_width
    spread[...] = jnp.where((lane >= row) & (lane < row + group_width), 1.0, 0.0).astype(BF16)

    pl.semaphore_wait(barrier, shards - 1 + xs - 1 + 1)

    def weight_copy(source, target, stage_no, to):
        return pltpu.make_async_remote_copy(
            src_ref=source, dst_ref=target, send_sem=ws_sem.at[stage_no], recv_sem=wr_sem.at[stage_no],
            device_id=to, device_id_type=MESH,
        )

    def drain(ref, sem):
        pltpu.make_async_copy(ref, ref, sem).wait()

    pltpu.make_async_copy(stage.at[g], full.at[s, g], wr_sem.at[0]).start()
    for step in range(zs - 1):
        dz = zigzag(zs // 2, step)
        weight_copy(stage.at[g], full.at[s, g], 0, (g, y * zs + (z + dz) % zs)).start()

    load.wait()

    def total(i, carry):
        part = x[pl.ds(pl.multiple_of(i * 64, 64), 64), :].astype(F32)
        return carry + fold_rows(part)

    zeros = jnp.zeros((ROWS, channels), F32)
    summed = lax.fori_loop(0, rows // 64, total, zeros)
    average = group_mean(jnp.sum(summed, axis=0, keepdims=True), collect, spread, members)

    def total_square(i, carry):
        part = x[pl.ds(pl.multiple_of(i * 64, 64), 64), :].astype(F32) - average
        return carry + fold_rows(part * part)

    summed = lax.fori_loop(0, rows // 64, total_square, zeros)
    variance = group_mean(jnp.sum(summed, axis=0, keepdims=True), collect, spread, members)
    stats[0:1, :] = average
    stats[1:2, :] = lax.rsqrt(variance + 1e-05) * gain_ref[...]
    stats[2:3, :] = shift_ref[...]

    def exchange(source, target, chunk, send_sem, recv_sem):
        pltpu.make_async_copy(source.at[chunk, s], target.at[chunk, s], recv_sem.at[chunk]).start()

        @pl.loop(0, shards - 1)
        def _(step):
            to = peer_of(step)
            pltpu.make_async_remote_copy(
                src_ref=source.at[chunk, to], dst_ref=target.at[chunk, s],
                send_sem=send_sem.at[chunk], recv_sem=recv_sem.at[chunk],
                device_id=(g, to), device_id_type=MESH,
            ).start()

    @pl.loop(0, chunks)
    def _(chunk):
        @pl.loop(0, strips // 2)
        def _(pair):
            for side in range(halves):
                lanes = pl.ds(pl.multiple_of(side * half + chunk * LANES, LANES), LANES)
                average = stats[0:1, lanes]
                scale = stats[1:2, lanes]
                shift = stats[2:3, lanes]
                upper, lower = [], []
                for block in range(blocks):
                    at = pl.ds(pl.multiple_of(block * BLOCK + pair * 16, 16), 16)
                    value = silu((x[at, lanes].astype(F32) - average) * scale + shift)
                    upper.append(value[0:ROWS])
                    lower.append(value[ROWS : 2 * ROWS])
                send1[chunk, side * strips + 2 * pair] = jnp.concatenate(upper, axis=0).astype(BF16)
                send1[chunk, side * strips + 2 * pair + 1] = jnp.concatenate(lower, axis=0).astype(BF16)

        exchange(send1, recv1, chunk, s1_sem, r1_sem)

    drain(full.at[pl.ds(0, zs), 0], wr_sem.at[0])
    mine = full.at[pl.ds(y * zs, zs), g]
    for step in range(ys - 1):
        dy = zigzag(ys // 2, step)
        weight_copy(mine, mine, 1, (g, ((y + dy) % ys) * zs + z)).start()

    def gather(chunk):
        drain(recv1.at[chunk], r1_sem.at[chunk])

        @pl.loop(0, shards)
        def _(view):
            table[pl.ds(view * blocks, blocks)] = recv1[chunk, view].astype(F32).reshape(blocks, ROWS, LANES)

        @pl.loop(0, shards)
        def _(view):
            parts = []
            for block in range(blocks):
                k = view * blocks + block
                count = count_ref[k]
                second = jnp.where(count > 1, 1.0, 0.0).astype(F32)
                third = jnp.where(count > 2, 1.0, 0.0).astype(F32)
                share = jnp.where(count > 2, 1.0 / 3.0, jnp.where(count > 1, 0.5, 1.0)).astype(F32)
                value = table[src_ref[k, 0]] + table[src_ref[k, 1]] * second + table[src_ref[k, 2]] * third
                parts.append(value * share)
            send2[chunk, view] = jnp.concatenate(parts, axis=0).astype(BF16)

        exchange(send2, recv2, chunk, s2_sem, r2_sem)

    gather(0)

    drain(full.at[pl.ds(0, (ys - 1) * zs), 0], wr_sem.at[1])
    mine = full.at[:, g]
    for step in range(xs - 1):
        dx = zigzag(xs // 2, step)
        weight_copy(mine, mine, 2, (((xx + dx) % xs) * cores + core, s)).start()
    weight_copy(mine, mine, 3, (sibling, s)).start()

    @pl.loop(1, chunks)
    def _(chunk):
        gather(chunk)

    drain(full.at[pl.ds(0, (xs - 1) * shards // pieces)], wr_sem.at[2])
    for dx in range(1, xs):
        theirs = full.at[:, ((xx + dx) % xs) * cores + core]
        weight_copy(theirs, theirs, 3, (sibling, s)).start()
    drain(full.at[pl.ds(0, xs * shards // pieces)], wr_sem.at[3])

    @pl.loop(0, shards)
    def _(shard):
        for piece in range(merge_pieces):
            at = pl.ds(pl.multiple_of(shard * merge_rows + piece * PIECE, PIECE), PIECE)
            pltpu.make_async_copy(full.at[shard, piece], merge_w.at[at], pack_sem).start()

    @pl.loop(0, shards // 2)
    def _(pair):
        parts = []
        for member in range(2):
            for piece in range(whole + 1):
                part = full[2 * pair + member, merge_pieces + piece].astype(F32)
                parts.append(part if piece < whole else part[0:rest])
        at = pl.ds(pl.multiple_of(pair * 2 * out_rows, PIECE), 2 * out_rows)
        out_w[at, :] = jnp.concatenate(parts, axis=0).astype(BF16)

    drain(merge_w, pack_sem)

    tile = 256
    tile_strips = tile // slice_rows
    tiles = rows // tile

    def left(ref, chunk_list, side, m):
        at = pl.ds(side * strips + m * tile_strips, tile_strips)
        return jnp.concatenate([ref[chunk, at].reshape(tile, LANES) for chunk in chunk_list], axis=1)

    @pl.loop(0, tiles)
    def _(m):
        sides = [left(send1, range(chunks), side, m) for side in range(halves)]
        at = pl.ds(pl.multiple_of(m * tile, tile), tile)
        acc[at, :] = jnp.dot(
            jnp.concatenate(sides, axis=1), merge_w[0:channels, :], preferred_element_type=F32
        )

    def add_epipolar(chunk_list, m):
        depth = len(chunk_list) * LANES
        first = chunk_list[0] * LANES
        sides = [left(recv2, chunk_list, side, m) for side in range(halves)]
        weights = [
            merge_w[channels + side * half + first : channels + side * half + first + depth, :]
            for side in range(halves)
        ]
        at = pl.ds(pl.multiple_of(m * tile, tile), tile)
        value = acc[at, :] + jnp.dot(
            jnp.concatenate(sides, axis=1), jnp.concatenate(weights, axis=0), preferred_element_type=F32
        )
        acc[at, :] = value
        return value

    first = 0
    while first < chunks - 1:
        group = list(range(first, min(first + 2, chunks - 1)))
        for chunk in group:
            drain(recv2.at[chunk], r2_sem.at[chunk])

        @pl.loop(0, tiles)
        def _(m):
            add_epipolar(group, m)

        first += len(group)

    drain(recv2.at[chunks - 1], r2_sem.at[chunks - 1])

    def last(m, carry):
        return carry + fold_rows(add_epipolar([chunks - 1], m))

    summed = lax.fori_loop(0, tiles, last, zeros)
    average2 = group_mean(jnp.sum(summed, axis=0, keepdims=True), collect, spread, members)

    def last_square(i, carry):
        part = acc[pl.ds(pl.multiple_of(i * 64, 64), 64), :] - average2
        return carry + fold_rows(part * part)

    summed = lax.fori_loop(0, rows // 64, last_square, zeros)
    variance2 = group_mean(jnp.sum(summed, axis=0, keepdims=True), collect, spread, members)
    stats[0:1, :] = average2
    stats[1:2, :] = lax.rsqrt(variance2 + 1e-05)

    @pl.loop(0, tiles)
    def _(m):
        at = pl.ds(pl.multiple_of(m * tile, tile), tile)
        value = silu((acc[at, :] - stats[0:1, :]) * stats[1:2, :]).astype(BF16)
        projected = jnp.dot(value, out_w[...], preferred_element_type=F32)
        for pair in range(tile_strips // 2):
            top = 2 * pair * slice_rows
            for block in range(blocks):
                both = jnp.concatenate(
                    [
                        projected[top + block * ROWS : top + (block + 1) * ROWS],
                        projected[top + slice_rows + block * ROWS : top + slice_rows + (block + 1) * ROWS],
                    ],
                    axis=0,
                )
                to = pl.ds(
                    pl.multiple_of(block * BLOCK + m * (tile_strips * ROWS) + pair * 16, 16), 16
                )
                x[to, :] = (x[to, :].astype(F32) + both).astype(BF16)
        for block in range(blocks):
            to = pl.ds(
                pl.multiple_of(block * BLOCK + m * (tile_strips * ROWS), tile_strips * ROWS), tile_strips * ROWS
            )
            pltpu.make_async_copy(x.at[to], out_hbm.at[to], out_sem).start()

    for chunk in range(chunks):
        drain(send1.at[chunk, pl.ds(0, shards - 1)], s1_sem.at[chunk])
        drain(send2.at[chunk, pl.ds(0, shards - 1)], s2_sem.at[chunk])
    drain(full.at[pl.ds(0, zs - 1), 0], ws_sem.at[0])
    drain(full.at[pl.ds(0, (ys - 1) * zs), 0], ws_sem.at[1])
    drain(full.at[pl.ds(0, (xs - 1) * shards // pieces)], ws_sem.at[2])
    drain(full.at[pl.ds(0, xs * shards // pieces)], ws_sem.at[3])
    drain(x, out_sem)


def solution(mesh):
    sizes = (4, 8, 4, 2)

    def per_device(features, norm_gain, norm_shift, merge_weight, out_weight, corr_src, corr_count):
        rows, channels = features.shape
        shards = lax.axis_size("shard")
        groups = lax.axis_size("grp")
        slice_rows = rows // BLOCK * ROWS
        chunks = channels // (shards // (BLOCK // ROWS)) // LANES
        vmem = pl.BlockSpec(memory_space=pltpu.VMEM)
        smem = pl.BlockSpec(memory_space=pltpu.SMEM)
        hbm = pl.BlockSpec(memory_space=pl.ANY)
        slices = pltpu.VMEM((chunks, shards, slice_rows, LANES), BF16)
        dma = pltpu.SemaphoreType.DMA
        return pl.pallas_call(
            functools.partial(kernel, sizes),
            out_shape=jax.ShapeDtypeStruct(features.shape, features.dtype),
            in_specs=[hbm, vmem, vmem, vmem, vmem, smem, smem],
            out_specs=hbm,
            scratch_shapes=[
                pltpu.VMEM((rows, channels), BF16),
                pltpu.VMEM((groups, PIECE, channels), BF16),
                slices, slices, slices, slices,
                pltpu.VMEM((corr_src.shape[0], ROWS, LANES), F32),
                pltpu.VMEM((shards, groups, PIECE, channels), BF16),
                pltpu.VMEM((2 * channels, channels), BF16),
                pltpu.VMEM((channels, channels), BF16),
                pltpu.VMEM((rows, channels), F32),
                pltpu.VMEM((channels, LANES), BF16),
                pltpu.VMEM((LANES, channels), BF16),
                pltpu.VMEM((ROWS, channels), F32),
                dma, dma, dma,
                dma((chunks,)), dma((chunks,)), dma((chunks,)), dma((chunks,)),
                dma((4,)), dma((4,)),
            ],
            compiler_params=pltpu.CompilerParams(
                collective_id=0, has_side_effects=True, vmem_limit_bytes=60 * 1024 * 1024
            ),
            name="merge_block",
        )(
            features, norm_gain.reshape(1, channels), norm_shift.reshape(1, channels),
            merge_weight, out_weight, corr_src, corr_count,
        )

    placed = (
        P(("grp", "shard"), None),
        P(),
        P(),
        P("shard", None),
        P("shard", None),
        P("grp", None),
        P("grp"),
    )
    return jax.shard_map(
        per_device, mesh=mesh, in_specs=placed, out_specs=P(("grp", "shard"), None), check_vma=False
    )
```

time: 253 us -> 154 us (0.61); the launches traced: 249 us -> 153 us
  Pallas kernels: 0 us -> 146 us
  waiting for transfers between devices: 138 us -> 0 us
  local copies, waits for them, and re-layouts: 37.5 us -> 7.46 us
  starting transfers between devices: 22.5 us -> 0 us
  matrix products: 21.3 us -> 0 us
  other arithmetic: 16.3 us -> 0 us
  between operations: 13.6 us -> 0.01 us
    pallas_call x0 -> x1, Pallas kernels: none -> 146 us  [per_device(): pl.pallas_call(functools.partial(kernel, sizes), out_shape=jax.ShapeDtype...]
    all_to_all x2 -> x0, waiting for transfers between devices: 137 us -> none  [the longest x1 74 us: per_device(): lax.all_to_all(slices, 'shard', split_axis=0, concat_axis=0, tiled=True)]
    all_to_all x2 -> x0, starting transfers between devices: 22.2 us -> none  [the longest x1 12.2 us: per_device(): lax.all_to_all(slices, 'shard', split_axis=0, concat_axis=0, tiled=True)]
    dot_general x2 -> x0, matrix products: 21.3 us -> none  [the longest x1 12 us: per_device(): jnp.dot(joined, lax.all_gather(merge_weight, 'shard', axis=0, tiled=True)...]
    reshape x4 -> x2, local copies, waits for them, and re-layouts: 15.4 us -> 2.58 us  [the longest x1 1.29 us: per_device(): norm_shift.reshape(1, channels)]
    gather x3 -> x0, local copies, waits for them, and re-layouts: 12.7 us -> none  [per_device(): picked = jnp.take(arrived, corr_src[:, position], axis=0, mode='clip')]
    reduce_sum x7 -> x0, other arithmetic: 8.44 us -> none  [the longest x4 5.96 us: group_norm(): jnp.sum(centered * centered, axis=(0, 2), keepdims=True) / members]
    convert_element_type x4 -> x0, other arithmetic: 7.77 us -> none  [the longest x1 4.47 us: per_device(): (summed / divisor).astype(jnp.bfloat16)]
  transfers between devices with their start and end apart: 4 -> 0, of which waited for: 2 -> 0; matrix products, arithmetic and copies ran while one was open for 26% -> 0% of each run, Pallas kernels for 0% -> 0%
where the time goes in v2:
time: 154 us; the launch traced here: 153 us
  Pallas kernels  146 us (95%)
  local copies, waits for them, and re-layouts  7.46 us (5%)
    pallas_call x1, Pallas kernels, per_device(): pl.pallas_call(functools.partial(kernel, sizes), out_shape=jax.ShapeDtype...  146 us
    unnamed x2, local copies, waits for them, and re-layouts  4.88 us

profile of v2, /device:TPU:1, one launch (start us, length us, event | category | flops | bytes accessed | tf_op | source)
XLA Modules:
  0.0 153.5 jit_solution(7717456272902115257)
XLA Ops:
  0.0 1.3 reshape.6.gain_ref
  1.3 1.3 reshape.7.shift_ref
  2.6 1.5 copy.8.src_ref
  4.1 146.0 %merge_block.1 = bf16[1024,1280]{1,0:T(8,128)(2,1)} custom-call(bf16[1024,1280]{1,0:T(8,128)(2,1)} %x_hbm.1, f32[1,1280]{1,0:T(1,128)} %reshape.6.gain_ref, f32[1,1280]{1,0:T(1,128)} %reshape.7.shift_ref, bf16[80,1280]{1,0:T(8,128)(2,1)} %merge_ref.1, bf16[40,1280]{1,0:T(8,128)(2,1)} %outw_ref.1, s32[256,3]{1,0:T(8,128)} %copy.8.src_ref, s32[256]{0:T(256)} %count_ref.1), custom_call_target="tpu_custom_call" | custom-call | tf_op jit(solution)/shard_map/merge_block/pallas_call | solution.py:357
  150.1 3.4 %copy.10 = bf16[1024,1280]{1,0:T(8,128)(2,1)} copy(bf16[1024,1280]{1,0:T(8,128)(2,1)} %merge_block.1) | data formatting | bytes 5242880

commit v3 on v2

--- a/solution.py
+++ b/solution.py
@@ -43,14 +43,15 @@
 
 
 def silu(values):
-    return values / (1.0 + jnp.exp(-values))
+    middle = 0.5 * values
+    return middle + middle * jnp.tanh(middle)
 
 
 def kernel(
     sizes,
-    x_hbm, gain_ref, shift_ref, merge_ref, outw_ref, src_ref, count_ref,
+    x_hbm, gain_hbm, shift_hbm, merge_hbm, outw_hbm, src_hbm, count_hbm,
     out_hbm,
-    x, stage, send1, recv1, send2, recv2, table, full, merge_w, out_w, acc, collect, spread, stats,
+    x, params, merge_ref, outw_ref, src_ref, count_ref, stage, send1, recv1, send2, recv2, table, full, merge_w, out_w, acc, collect, spread, stats,
     load_sem, out_sem, pack_sem, s1_sem, r1_sem, s2_sem, r2_sem, ws_sem, wr_sem,
 ):
     ys, zs, xs, cores = sizes
@@ -74,8 +75,19 @@
     y, z = s // zs, s % zs
     xx, core = g // cores, g % cores
 
-    load = pltpu.make_async_copy(x_hbm, x, load_sem)
+    load = pltpu.make_async_copy(x_hbm, x, load_sem.at[0])
     load.start()
+    fetches = [
+        pltpu.make_async_copy(source, target, load_sem.at[1 + i])
+        for i, (source, target) in enumerate(
+            (
+                (merge_hbm, merge_ref), (outw_hbm, outw_ref), (gain_hbm, params.at[0]), (shift_hbm, params.at[1]),
+                (src_hbm, src_ref), (count_hbm, count_ref),
+            )
+        )
+    ]
+    for fetch in fetches:
+        fetch.start()
 
     def peer_of(step):
         dz = zigzag(zs // 2, step // ys)
@@ -93,17 +105,6 @@
         pl.semaphore_signal(barrier, inc=1, device_id=(to, s), device_id_type=MESH)
     sibling = xx * cores + (core + 1) % cores
     pl.semaphore_signal(barrier, inc=1, device_id=(sibling, s), device_id_type=MESH)
-
-    for piece in range(merge_pieces):
-        stage[piece] = merge_ref[piece * PIECE : (piece + 1) * PIECE, :]
-    whole = out_rows // PIECE
-    for piece in range(whole):
-        stage[merge_pieces + piece] = outw_ref[piece * PIECE : (piece + 1) * PIECE, :]
-    rest = out_rows - whole * PIECE
-    tail = outw_ref[whole * PIECE : out_rows, :].astype(F32)
-    stage[merge_pieces + whole] = jnp.concatenate(
-        [tail, jnp.zeros((PIECE - rest, channels), F32)], axis=0
-    ).astype(BF16)
 
     lane = lax.broadcasted_iota(jnp.int32, (channels, LANES), 1) * group_width
     row = lax.broadcasted_iota(jnp.int32, (channels, LANES), 0)
@@ -112,8 +113,6 @@
     row = lax.broadcasted_iota(jnp.int32, (LANES, channels), 0) * group_width
     spread[...] = jnp.where((lane >= row) & (lane < row + group_width), 1.0, 0.0).astype(BF16)
 
-    pl.semaphore_wait(barrier, shards - 1 + xs - 1 + 1)
-
     def weight_copy(source, target, stage_no, to):
         return pltpu.make_async_remote_copy(
             src_ref=source, dst_ref=target, send_sem=ws_sem.at[stage_no], recv_sem=wr_sem.at[stage_no],
@@ -123,11 +122,6 @@
     def drain(ref, sem):
         pltpu.make_async_copy(ref, ref, sem).wait()
 
-    pltpu.make_async_copy(stage.at[g], full.at[s, g], wr_sem.at[0]).start()
-    for step in range(zs - 1):
-        dz = zigzag(zs // 2, step)
-        weight_copy(stage.at[g], full.at[s, g], 0, (g, y * zs + (z + dz) % zs)).start()
-
     load.wait()
 
     def total(i, carry):
@@ -145,8 +139,10 @@
     summed = lax.fori_loop(0, rows // 64, total_square, zeros)
     variance = group_mean(jnp.sum(summed, axis=0, keepdims=True), collect, spread, members)
     stats[0:1, :] = average
-    stats[1:2, :] = lax.rsqrt(variance + 1e-05) * gain_ref[...]
-    stats[2:3, :] = shift_ref[...]
+    fetches[2].wait()
+    fetches[3].wait()
+    stats[1:2, :] = lax.rsqrt(variance + 1e-05) * params[0:1, :]
+    stats[2:3, :] = params[1:2, :]
 
     def exchange(source, target, chunk, send_sem, recv_sem):
         pltpu.make_async_copy(source.at[chunk, s], target.at[chunk, s], recv_sem.at[chunk]).start()
@@ -160,8 +156,7 @@
                 device_id=(g, to), device_id_type=MESH,
             ).start()
 
-    @pl.loop(0, chunks)
-    def _(chunk):
+    def hide(chunk):
         @pl.loop(0, strips // 2)
         def _(pair):
             for side in range(halves):
@@ -178,6 +173,33 @@
                 send1[chunk, side * strips + 2 * pair] = jnp.concatenate(upper, axis=0).astype(BF16)
                 send1[chunk, side * strips + 2 * pair + 1] = jnp.concatenate(lower, axis=0).astype(BF16)
 
+    fetches[0].wait()
+    fetches[1].wait()
+
+    for piece in range(merge_pieces):
+        stage[piece] = merge_ref[piece * PIECE : (piece + 1) * PIECE, :]
+    whole = out_rows // PIECE
+    for piece in range(whole):
+        stage[merge_pieces + piece] = outw_ref[piece * PIECE : (piece + 1) * PIECE, :]
+    rest = out_rows - whole * PIECE
+    tail = outw_ref[whole * PIECE : out_rows, :].astype(F32)
+    stage[merge_pieces + whole] = jnp.concatenate(
+        [tail, jnp.zeros((PIECE - rest, channels), F32)], axis=0
+    ).astype(BF16)
+
+    hide(0)
+    pl.semaphore_wait(barrier, shards - 1 + xs - 1 + 1)
+
+    pltpu.make_async_copy(stage.at[g], full.at[s, g], wr_sem.at[0]).start()
+    for step in range(zs - 1):
+        dz = zigzag(zs // 2, step)
+        weight_copy(stage.at[g], full.at[s, g], 0, (g, y * zs + (z + dz) % zs)).start()
+
+    exchange(send1, recv1, 0, s1_sem, r1_sem)
+
+    @pl.loop(1, chunks)
+    def _(chunk):
+        hide(chunk)
         exchange(send1, recv1, chunk, s1_sem, r1_sem)
 
     drain(full.at[pl.ds(0, zs), 0], wr_sem.at[0])
@@ -202,12 +224,14 @@
                 second = jnp.where(count > 1, 1.0, 0.0).astype(F32)
                 third = jnp.where(count > 2, 1.0, 0.0).astype(F32)
                 share = jnp.where(count > 2, 1.0 / 3.0, jnp.where(count > 1, 0.5, 1.0)).astype(F32)
-                value = table[src_ref[k, 0]] + table[src_ref[k, 1]] * second + table[src_ref[k, 2]] * third
+                value = table[src_ref[0, k]] + table[src_ref[1, k]] * second + table[src_ref[2, k]] * third
                 parts.append(value * share)
             send2[chunk, view] = jnp.concatenate(parts, axis=0).astype(BF16)
 
         exchange(send2, recv2, chunk, s2_sem, r2_sem)
 
+    fetches[4].wait()
+    fetches[5].wait()
     gather(0)
 
     drain(full.at[pl.ds(0, (ys - 1) * zs), 0], wr_sem.at[1])
@@ -288,22 +312,23 @@
 
         first += len(group)
 
+    def partial(i, carry):
+        return carry + fold_rows(acc[pl.ds(pl.multiple_of(i * 64, 64), 64), :])
+
+    summed = lax.fori_loop(0, rows // 64, partial, zeros)
+    stats[0:1, :] = group_mean(jnp.sum(summed, axis=0, keepdims=True), collect, spread, members)
+
     drain(recv2.at[chunks - 1], r2_sem.at[chunks - 1])
 
     def last(m, carry):
-        return carry + fold_rows(add_epipolar([chunks - 1], m))
-
-    summed = lax.fori_loop(0, tiles, last, zeros)
-    average2 = group_mean(jnp.sum(summed, axis=0, keepdims=True), collect, spread, members)
-
-    def last_square(i, carry):
-        part = acc[pl.ds(pl.multiple_of(i * 64, 64), 64), :] - average2
-        return carry + fold_rows(part * part)
-
-    summed = lax.fori_loop(0, rows // 64, last_square, zeros)
-    variance2 = group_mean(jnp.sum(summed, axis=0, keepdims=True), collect, spread, members)
-    stats[0:1, :] = average2
-    stats[1:2, :] = lax.rsqrt(variance2 + 1e-05)
+        difference = add_epipolar([chunks - 1], m) - stats[0:1, :]
+        return carry[0] + fold_rows(difference), carry[1] + fold_rows(difference * difference)
+
+    summed, squares = lax.fori_loop(0, tiles, last, (zeros, zeros))
+    moved = group_mean(jnp.sum(summed, axis=0, keepdims=True), collect, spread, members)
+    square = group_mean(jnp.sum(squares, axis=0, keepdims=True), collect, spread, members)
+    stats[0:1, :] = stats[0:1, :] + moved
+    stats[1:2, :] = lax.rsqrt(jnp.maximum(square - moved * moved, 0.0) + 1e-05)
 
     @pl.loop(0, tiles)
     def _(m):
@@ -349,18 +374,21 @@
         groups = lax.axis_size("grp")
         slice_rows = rows // BLOCK * ROWS
         chunks = channels // (shards // (BLOCK // ROWS)) // LANES
-        vmem = pl.BlockSpec(memory_space=pltpu.VMEM)
-        smem = pl.BlockSpec(memory_space=pltpu.SMEM)
-        hbm = pl.BlockSpec(memory_space=pl.ANY)
+        hbm = pl.BlockSpec(memory_space=pltpu.HBM)
         slices = pltpu.VMEM((chunks, shards, slice_rows, LANES), BF16)
         dma = pltpu.SemaphoreType.DMA
         return pl.pallas_call(
             functools.partial(kernel, sizes),
             out_shape=jax.ShapeDtypeStruct(features.shape, features.dtype),
-            in_specs=[hbm, vmem, vmem, vmem, vmem, smem, smem],
-            out_specs=hbm,
+            in_specs=[hbm] * 7,
+            out_specs=pl.BlockSpec(memory_space=pl.ANY),
             scratch_shapes=[
                 pltpu.VMEM((rows, channels), BF16),
+                pltpu.VMEM((ROWS, channels), F32),
+                pltpu.VMEM(merge_weight.shape, BF16),
+                pltpu.VMEM(out_weight.shape, BF16),
+                pltpu.SMEM(corr_src.shape[::-1], jnp.int32),
+                pltpu.SMEM(corr_count.shape, jnp.int32),
                 pltpu.VMEM((groups, PIECE, channels), BF16),
                 slices, slices, slices, slices,
                 pltpu.VMEM((corr_src.shape[0], ROWS, LANES), F32),
@@ -371,17 +399,21 @@
                 pltpu.VMEM((channels, LANES), BF16),
                 pltpu.VMEM((LANES, channels), BF16),
                 pltpu.VMEM((ROWS, channels), F32),
-                dma, dma, dma,
+                dma((7,)), dma, dma,
                 dma((chunks,)), dma((chunks,)), dma((chunks,)), dma((chunks,)),
                 dma((4,)), dma((4,)),
             ],
             compiler_params=pltpu.CompilerParams(
-                collective_id=0, has_side_effects=True, vmem_limit_bytes=60 * 1024 * 1024
+                collective_id=0, has_side_effects=True, vmem_limit_bytes=44 * 1024 * 1024
             ),
             name="merge_block",
         )(
-            features, norm_gain.reshape(1, channels), norm_shift.reshape(1, channels),
-            merge_weight, out_weight, corr_src, corr_count,
+            *(
+                pltpu.with_memory_space_constraint(array, pltpu.HBM)
+                for array in (
+                    features, norm_gain, norm_shift, merge_weight, out_weight, corr_src.T, corr_count
+                )
+            )
         )
 
     placed = (

time: 154 us -> 145 us (0.942)
  local copies, waits for them, and re-layouts: 7.46 us -> 1.49 us
  Pallas kernels: 146 us -> 143 us
    unnamed x2 -> x1, local copies, waits for them, and re-layouts: 4.88 us -> 1.49 us
    reshape x2 -> x0, local copies, waits for them, and re-layouts: 2.58 us -> none  [the longest x1 1.29 us: per_device(): norm_shift.reshape(1, channels)]
    pallas_call x1, Pallas kernels: 146 us -> 143 us  [per_device(): pl.pallas_call(functools.partial(kernel, sizes), out_shape=jax.ShapeDtype...]
where the time goes in v3:
time: 145 us
  Pallas kernels  143 us (99%)
  local copies, waits for them, and re-layouts  1.49 us (1%)
    pallas_call x1, Pallas kernels, per_device(): pl.pallas_call(functools.partial(kernel, sizes), out_shape=jax.ShapeDtype...  143 us

profile of v3, /device:TPU:1, one launch (start us, length us, event | category | flops | bytes accessed | tf_op | source)
XLA Modules:
  0.0 144.9 jit_solution(1909516723861743977)
XLA Ops:
  0.0 143.4 %merge_block.1 = bf16[1024,1280]{1,0:T(8,128)(2,1)S(1)} custom-call(bf16[1024,1280]{1,0:T(8,128)(2,1)} %x_hbm.1, f32[1280]{0:T(1024)} %gain_hbm.1, f32[1280]{0:T(1024)} %shift_hbm.1, bf16[80,1280]{1,0:T(8,128)(2,1)} %merge_hbm.1, bf16[40,1280]{1,0:T(8,128)(2,1)} %outw_hbm.1, s32[3,256]{1,0:T(4,128)} %bitcast.1, s32[256]{0:T(256)} %count_hbm.1), custom_call_target="tpu_custom_call" | custom-call | tf_op jit(solution)/shard_map/merge_block/pallas_call | solution.py:380
  143.4 1.5 %copy.9 = bf16[1024,1280]{1,0:T(8,128)(2,1)} copy(bf16[1024,1280]{1,0:T(8,128)(2,1)S(1)} %merge_block.1) | data formatting | bytes 5242880

commit v4 on v3

--- a/solution.py
+++ b/solution.py
@@ -22,20 +22,22 @@
     return center + (1 - odd) * (place // 2) - odd * ((place + 1) // 2)
 
 
-def split_rows(row):
-    high = row.astype(BF16).astype(F32)
-    rest = row - high
-    middle = rest.astype(BF16).astype(F32)
-    low = rest - middle
-    fill = jnp.zeros((PIECE - 3, row.shape[1]), F32)
-    return jnp.concatenate([high, middle, low, fill], axis=0).astype(BF16)
+def exact_rows(rows, matrix):
+    parts = []
+    for row in rows:
+        high = row.astype(BF16).astype(F32)
+        rest = row - high
+        middle = rest.astype(BF16).astype(F32)
+        parts += [high, middle, rest - middle]
+    parts.append(jnp.zeros((PIECE - len(parts), rows[0].shape[1]), F32))
+    stacked = jnp.concatenate(parts, axis=0).astype(BF16)
+    product = jnp.dot(stacked, matrix[...], preferred_element_type=F32)
+    return [product[i : i + 1] + product[i + 1 : i + 2] + product[i + 2 : i + 3] for i in range(0, 3 * len(rows), 3)]
 
 
 def group_mean(row, collect, spread, members):
-    parts = jnp.dot(split_rows(row), collect[...], preferred_element_type=F32)
-    mean = (parts[0:1] + parts[1:2] + parts[2:3]) / members
-    parts = jnp.dot(split_rows(mean), spread[...], preferred_element_type=F32)
-    return parts[0:1] + parts[1:2] + parts[2:3]
+    (total,) = exact_rows([row], collect)
+    return exact_rows([total / members], spread)[0]
 
 
 def fold_rows(values):
@@ -50,9 +52,9 @@
 def kernel(
     sizes,
     x_hbm, gain_hbm, shift_hbm, merge_hbm, outw_hbm, src_hbm, count_hbm,
-    out_hbm,
-    x, params, merge_ref, outw_ref, src_ref, count_ref, stage, send1, recv1, send2, recv2, table, full, merge_w, out_w, acc, collect, spread, stats,
-    load_sem, out_sem, pack_sem, s1_sem, r1_sem, s2_sem, r2_sem, ws_sem, wr_sem,
+    out_ref,
+    x, params, merge_ref, outw_ref, src_ref, count_ref, stage, send1, recv1, send2, recv2, table, full, merge_w, out_w, acc, act, collect, spread, stats,
+    load_sem, s1_sem, r1_sem, s2_sem, r2_sem, ws_sem, wr_sem,
 ):
     ys, zs, xs, cores = sizes
     shards = ys * zs
@@ -255,7 +257,7 @@
     def _(shard):
         for piece in range(merge_pieces):
             at = pl.ds(pl.multiple_of(shard * merge_rows + piece * PIECE, PIECE), PIECE)
-            pltpu.make_async_copy(full.at[shard, piece], merge_w.at[at], pack_sem).start()
+            merge_w[at, :] = full[shard, piece]
 
     @pl.loop(0, shards // 2)
     def _(pair):
@@ -266,8 +268,6 @@
                 parts.append(part if piece < whole else part[0:rest])
         at = pl.ds(pl.multiple_of(pair * 2 * out_rows, PIECE), 2 * out_rows)
         out_w[at, :] = jnp.concatenate(parts, axis=0).astype(BF16)
-
-    drain(merge_w, pack_sem)
 
     tile = 256
     tile_strips = tile // slice_rows
@@ -320,40 +320,61 @@
 
     drain(recv2.at[chunks - 1], r2_sem.at[chunks - 1])
 
-    def last(m, carry):
-        difference = add_epipolar([chunks - 1], m) - stats[0:1, :]
-        return carry[0] + fold_rows(difference), carry[1] + fold_rows(difference * difference)
-
-    summed, squares = lax.fori_loop(0, tiles, last, (zeros, zeros))
-    moved = group_mean(jnp.sum(summed, axis=0, keepdims=True), collect, spread, members)
-    square = group_mean(jnp.sum(squares, axis=0, keepdims=True), collect, spread, members)
-    stats[0:1, :] = stats[0:1, :] + moved
-    stats[1:2, :] = lax.rsqrt(jnp.maximum(square - moved * moved, 0.0) + 1e-05)
-
-    @pl.loop(0, tiles)
-    def _(m):
-        at = pl.ds(pl.multiple_of(m * tile, tile), tile)
-        value = silu((acc[at, :] - stats[0:1, :]) * stats[1:2, :]).astype(BF16)
-        projected = jnp.dot(value, out_w[...], preferred_element_type=F32)
-        for pair in range(tile_strips // 2):
-            top = 2 * pair * slice_rows
-            for block in range(blocks):
-                both = jnp.concatenate(
-                    [
-                        projected[top + block * ROWS : top + (block + 1) * ROWS],
-                        projected[top + slice_rows + block * ROWS : top + slice_rows + (block + 1) * ROWS],
-                    ],
-                    axis=0,
-                )
-                to = pl.ds(
-                    pl.multiple_of(block * BLOCK + m * (tile_strips * ROWS) + pair * 16, 16), 16
-                )
-                x[to, :] = (x[to, :].astype(F32) + both).astype(BF16)
-        for block in range(blocks):
-            to = pl.ds(
-                pl.multiple_of(block * BLOCK + m * (tile_strips * ROWS), tile_strips * ROWS), tile_strips * ROWS
-            )
-            pltpu.make_async_copy(x.at[to], out_hbm.at[to], out_sem).start()
+    width = 256
+    spans = channels // width
+    lasts = [left(recv2, [chunks - 1], side, m) for m in range(tiles) for side in range(halves)]
+    first = (chunks - 1) * LANES
+    sums = []
+    for n in range(spans):
+        columns = slice(n * width, (n + 1) * width)
+        weights = [
+            merge_w[channels + side * half + first : channels + side * half + first + LANES, columns]
+            for side in range(halves)
+        ]
+        weights = jnp.concatenate(weights, axis=0)
+        middle = stats[0:1, columns]
+        summed = jnp.zeros((ROWS, width), F32)
+        squares = jnp.zeros((ROWS, width), F32)
+        for m in range(tiles):
+            at = slice(m * tile, (m + 1) * tile)
+            inputs = jnp.concatenate(lasts[halves * m : halves * (m + 1)], axis=1)
+            difference = acc[at, columns] - middle + jnp.dot(inputs, weights, preferred_element_type=F32)
+            acc[at, columns] = difference
+            summed = summed + fold_rows(difference)
+            squares = squares + fold_rows(difference * difference)
+        sums.append((summed, squares))
+    rows_of = [
+        jnp.sum(jnp.concatenate([pair[i] for pair in sums], axis=1), axis=0, keepdims=True) for i in range(2)
+    ]
+    moved, square = [total / members for total in exact_rows(rows_of, collect)]
+    scale = lax.rsqrt(jnp.maximum(square - moved * moved, 0.0) + 1e-05)
+    moved, scale = exact_rows([moved, scale], spread)
+    stats[0:1, :] = moved
+    stats[1:2, :] = scale
+
+    def activate(m, n):
+        at, columns = slice(m * tile, (m + 1) * tile), slice(n * width, (n + 1) * width)
+        value = silu((acc[at, columns] - stats[0:1, columns]) * stats[1:2, columns])
+        act[at, columns] = value.astype(BF16)
+
+    for n in range(spans):
+        activate(0, n)
+    for m in range(tiles):
+        at = slice(m * tile, (m + 1) * tile)
+        for n in range(spans):
+            columns = slice(n * width, (n + 1) * width)
+            projected = jnp.dot(act[at, :], out_w[:, columns], preferred_element_type=F32)
+            if m + 1 < tiles:
+                activate(m + 1, n)
+            for pair in range(tile_strips // 2):
+                top = 2 * pair * slice_rows
+                for block in range(blocks):
+                    upper = projected[top + block * ROWS : top + (block + 1) * ROWS]
+                    lower = projected[top + slice_rows + block * ROWS : top + slice_rows + (block + 1) * ROWS]
+                    start = block * BLOCK + m * (tile_strips * ROWS) + pair * 2 * ROWS
+                    to = slice(start, start + 2 * ROWS)
+                    value = x[to, columns].astype(F32) + jnp.concatenate([upper, lower], axis=0)
+                    out_ref[to, columns] = value.astype(BF16)
 
     for chunk in range(chunks):
         drain(send1.at[chunk, pl.ds(0, shards - 1)], s1_sem.at[chunk])
@@ -362,7 +383,6 @@
     drain(full.at[pl.ds(0, (ys - 1) * zs), 0], ws_sem.at[1])
     drain(full.at[pl.ds(0, (xs - 1) * shards // pieces)], ws_sem.at[2])
     drain(full.at[pl.ds(0, xs * shards // pieces)], ws_sem.at[3])
-    drain(x, out_sem)
 
 
 def solution(mesh):
@@ -379,9 +399,9 @@
         dma = pltpu.SemaphoreType.DMA
         return pl.pallas_call(
             functools.partial(kernel, sizes),
-            out_shape=jax.ShapeDtypeStruct(features.shape, features.dtype),
+            out_shape=pltpu.VMEM(features.shape, features.dtype),
             in_specs=[hbm] * 7,
-            out_specs=pl.BlockSpec(memory_space=pl.ANY),
+            out_specs=pl.BlockSpec(memory_space=pltpu.VMEM),
             scratch_shapes=[
                 pltpu.VMEM((rows, channels), BF16),
                 pltpu.VMEM((ROWS, channels), F32),
@@ -396,10 +416,11 @@
                 pltpu.VMEM((2 * channels, channels), BF16),
                 pltpu.VMEM((channels, channels), BF16),
                 pltpu.VMEM((rows, channels), F32),
+                pltpu.VMEM((rows, channels), BF16),
                 pltpu.VMEM((channels, LANES), BF16),
                 pltpu.VMEM((LANES, channels), BF16),
                 pltpu.VMEM((ROWS, channels), F32),
-                dma((7,)), dma, dma,
+                dma((7,)),
                 dma((chunks,)), dma((chunks,)), dma((chunks,)), dma((chunks,)),
                 dma((4,)), dma((4,)),
             ],

time: 145 us -> 140 us (0.966)
  Pallas kernels: 143 us -> 138 us
    pallas_call x1, Pallas kernels: 143 us -> 138 us  [per_device(): pl.pallas_call(functools.partial(kernel, sizes), out_shape=pltpu.VMEM(fea...]
where the time goes in v4:
time: 140 us; the launch traced here: 139 us
  Pallas kernels  138 us (99%)
  local copies, waits for them, and re-layouts  1.49 us (1%)
    pallas_call x1, Pallas kernels, per_device(): pl.pallas_call(functools.partial(kernel, sizes), out_shape=pltpu.VMEM(fea...  138 us

profile of v4, /device:TPU:1, one launch (start us, length us, event | category | flops | bytes accessed | tf_op | source)
XLA Modules:
  0.0 139.2 jit_solution(17841767865316141227)
XLA Ops:
  0.0 137.7 %merge_block.1 = bf16[1024,1280]{1,0:T(8,128)(2,1)S(1)} custom-call(bf16[1024,1280]{1,0:T(8,128)(2,1)} %x_hbm.1, f32[1280]{0:T(1024)} %gain_hbm.1, f32[1280]{0:T(1024)} %shift_hbm.1, bf16[80,1280]{1,0:T(8,128)(2,1)} %merge_hbm.1, bf16[40,1280]{1,0:T(8,128)(2,1)} %outw_hbm.1, s32[3,256]{1,0:T(4,128)} %bitcast.1, s32[256]{0:T(256)} %count_hbm.1), custom_call_target="tpu_custom_call" | custom-call | tf_op jit(solution)/shard_map/merge_block/pallas_call | solution.py:400
  137.7 1.5 %copy.9 = bf16[1024,1280]{1,0:T(8,128)(2,1)} copy(bf16[1024,1280]{1,0:T(8,128)(2,1)S(1)} %merge_block.1) | data formatting | bytes 5242880

commit v5 on v4

--- a/solution.py
+++ b/solution.py
@@ -146,10 +146,11 @@
     stats[1:2, :] = lax.rsqrt(variance + 1e-05) * params[0:1, :]
     stats[2:3, :] = params[1:2, :]
 
-    def exchange(source, target, chunk, send_sem, recv_sem):
+    def own_slice(source, target, chunk, recv_sem):
         pltpu.make_async_copy(source.at[chunk, s], target.at[chunk, s], recv_sem.at[chunk]).start()
 
-        @pl.loop(0, shards - 1)
+    def exchange(source, target, chunk, send_sem, recv_sem, start, stop):
+        @pl.loop(start, stop)
         def _(step):
             to = peer_of(step)
             pltpu.make_async_remote_copy(
@@ -192,19 +193,34 @@
     hide(0)
     pl.semaphore_wait(barrier, shards - 1 + xs - 1 + 1)
 
+    def beside(dz):
+        return y * zs + (z + dz + zs) % zs
+
     pltpu.make_async_copy(stage.at[g], full.at[s, g], wr_sem.at[0]).start()
-    for step in range(zs - 1):
-        dz = zigzag(zs // 2, step)
-        weight_copy(stage.at[g], full.at[s, g], 0, (g, y * zs + (z + dz) % zs)).start()
-
-    exchange(send1, recv1, 0, s1_sem, r1_sem)
+    for dz in (-2, 2, -1, 1):
+        weight_copy(stage.at[g], full.at[s, g], 0, (g, beside(dz))).start()
+
+    early = shards // 4
+    own_slice(send1, recv1, 0, r1_sem)
+    exchange(send1, recv1, 0, s1_sem, r1_sem, 0, early)
+
+    drain(full.at[pl.ds(0, 5), 0], wr_sem.at[0])
+    way = 1 - 2 * core
+    onward = full.at[beside(-2 * way), g]
+    weight_copy(onward, onward, 4, (g, beside(2 * way))).start()
+    for dz in (-1, 1):
+        onward = full.at[beside(-2 * dz), g]
+        weight_copy(onward, onward, 4, (g, beside(dz))).start()
+
+    exchange(send1, recv1, 0, s1_sem, r1_sem, early, shards - 1)
 
     @pl.loop(1, chunks)
     def _(chunk):
         hide(chunk)
-        exchange(send1, recv1, chunk, s1_sem, r1_sem)
-
-    drain(full.at[pl.ds(0, zs), 0], wr_sem.at[0])
+        own_slice(send1, recv1, chunk, r1_sem)
+        exchange(send1, recv1, chunk, s1_sem, r1_sem, 0, shards - 1)
+
+    drain(full.at[pl.ds(0, 3), 0], wr_sem.at[4])
     mine = full.at[pl.ds(y * zs, zs), g]
     for step in range(ys - 1):
         dy = zigzag(ys // 2, step)
@@ -230,7 +246,8 @@
                 parts.append(value * share)
             send2[chunk, view] = jnp.concatenate(parts, axis=0).astype(BF16)
 
-        exchange(send2, recv2, chunk, s2_sem, r2_sem)
+        own_slice(send2, recv2, chunk, r2_sem)
+        exchange(send2, recv2, chunk, s2_sem, r2_sem, 0, shards - 1)
 
     fetches[4].wait()
     fetches[5].wait()
@@ -379,7 +396,8 @@
     for chunk in range(chunks):
         drain(send1.at[chunk, pl.ds(0, shards - 1)], s1_sem.at[chunk])
         drain(send2.at[chunk, pl.ds(0, shards - 1)], s2_sem.at[chunk])
-    drain(full.at[pl.ds(0, zs - 1), 0], ws_sem.at[0])
+    drain(full.at[pl.ds(0, 4), 0], ws_sem.at[0])
+    drain(full.at[pl.ds(0, 3), 0], ws_sem.at[4])
     drain(full.at[pl.ds(0, (ys - 1) * zs), 0], ws_sem.at[1])
     drain(full.at[pl.ds(0, (xs - 1) * shards // pieces)], ws_sem.at[2])
     drain(full.at[pl.ds(0, xs * shards // pieces)], ws_sem.at[3])
@@ -422,7 +440,7 @@
                 pltpu.VMEM((ROWS, channels), F32),
                 dma((7,)),
                 dma((chunks,)), dma((chunks,)), dma((chunks,)), dma((chunks,)),
-                dma((4,)), dma((4,)),
+                dma((5,)), dma((5,)),
             ],
             compiler_params=pltpu.CompilerParams(
                 collective_id=0, has_side_effects=True, vmem_limit_bytes=44 * 1024 * 1024

time: 140 us -> 137 us (0.979)
  Pallas kernels: 138 us -> 134 us
    pallas_call x1, Pallas kernels: 138 us -> 134 us  [per_device(): pl.pallas_call(functools.partial(kernel, sizes), out_shape=pltpu.VMEM(fea...]
where the time goes in v5:
time: 137 us; the launch traced here: 136 us
  Pallas kernels  134 us (98%)
  local copies, waits for them, and re-layouts  1.49 us (1%)
    pallas_call x1, Pallas kernels, per_device(): pl.pallas_call(functools.partial(kernel, sizes), out_shape=pltpu.VMEM(fea...  134 us

profile of v5, /device:TPU:1, one launch (start us, length us, event | category | flops | bytes accessed | tf_op | source)
XLA Modules:
  0.0 135.6 jit_solution(4349635275557626581)
XLA Ops:
  0.0 134.1 %merge_block.1 = bf16[1024,1280]{1,0:T(8,128)(2,1)S(1)} custom-call(bf16[1024,1280]{1,0:T(8,128)(2,1)} %x_hbm.1, f32[1280]{0:T(1024)} %gain_hbm.1, f32[1280]{0:T(1024)} %shift_hbm.1, bf16[80,1280]{1,0:T(8,128)(2,1)} %merge_hbm.1, bf16[40,1280]{1,0:T(8,128)(2,1)} %outw_hbm.1, s32[3,256]{1,0:T(4,128)} %bitcast.1, s32[256]{0:T(256)} %count_hbm.1), custom_call_target="tpu_custom_call" | custom-call | tf_op jit(solution)/shard_map/merge_block/pallas_call | solution.py:418
  134.1 1.5 %copy.9 = bf16[1024,1280]{1,0:T(8,128)(2,1)} copy(bf16[1024,1280]{1,0:T(8,128)(2,1)S(1)} %merge_block.1) | data formatting | bytes 5242880

commit v6 on v5

--- a/solution.py
+++ b/solution.py
@@ -124,6 +124,29 @@
     def drain(ref, sem):
         pltpu.make_async_copy(ref, ref, sem).wait()
 
+    fetches[0].wait()
+    fetches[1].wait()
+
+    for piece in range(merge_pieces):
+        stage[piece] = merge_ref[piece * PIECE : (piece + 1) * PIECE, :]
+    whole = out_rows // PIECE
+    for piece in range(whole):
+        stage[merge_pieces + piece] = outw_ref[piece * PIECE : (piece + 1) * PIECE, :]
+    rest = out_rows - whole * PIECE
+    tail = outw_ref[whole * PIECE : out_rows, :].astype(F32)
+    stage[merge_pieces + whole] = jnp.concatenate(
+        [tail, jnp.zeros((PIECE - rest, channels), F32)], axis=0
+    ).astype(BF16)
+
+    pl.semaphore_wait(barrier, shards - 1 + xs - 1 + 1)
+
+    def beside(dz):
+        return y * zs + (z + dz + zs) % zs
+
+    pltpu.make_async_copy(stage.at[g], full.at[s, g], wr_sem.at[0]).start()
+    for dz in (-2, 2, -1, 1):
+        weight_copy(stage.at[g], full.at[s, g], 0, (g, beside(dz))).start()
+
     load.wait()
 
     def total(i, carry):
@@ -176,30 +199,7 @@
                 send1[chunk, side * strips + 2 * pair] = jnp.concatenate(upper, axis=0).astype(BF16)
                 send1[chunk, side * strips + 2 * pair + 1] = jnp.concatenate(lower, axis=0).astype(BF16)
 
-    fetches[0].wait()
-    fetches[1].wait()
-
-    for piece in range(merge_pieces):
-        stage[piece] = merge_ref[piece * PIECE : (piece + 1) * PIECE, :]
-    whole = out_rows // PIECE
-    for piece in range(whole):
-        stage[merge_pieces + piece] = outw_ref[piece * PIECE : (piece + 1) * PIECE, :]
-    rest = out_rows - whole * PIECE
-    tail = outw_ref[whole * PIECE : out_rows, :].astype(F32)
-    stage[merge_pieces + whole] = jnp.concatenate(
-        [tail, jnp.zeros((PIECE - rest, channels), F32)], axis=0
-    ).astype(BF16)
-
     hide(0)
-    pl.semaphore_wait(barrier, shards - 1 + xs - 1 + 1)
-
-    def beside(dz):
-        return y * zs + (z + dz + zs) % zs
-
-    pltpu.make_async_copy(stage.at[g], full.at[s, g], wr_sem.at[0]).start()
-    for dz in (-2, 2, -1, 1):
-        weight_copy(stage.at[g], full.at[s, g], 0, (g, beside(dz))).start()
-
     early = shards // 4
     own_slice(send1, recv1, 0, r1_sem)
     exchange(send1, recv1, 0, s1_sem, r1_sem, 0, early)

time: 137 us -> 136 us (level); the launches traced: 136 us -> 136 us
  no operation moved by 1% of the time
where the time goes in v6:
time: 136 us
  Pallas kernels  135 us (99%)
  local copies, waits for them, and re-layouts  1.49 us (1%)
    pallas_call x1, Pallas kernels, per_device(): pl.pallas_call(functools.partial(kernel, sizes), out_shape=pltpu.VMEM(fea...  135 us

profile of v6, /device:TPU:1, one launch (start us, length us, event | category | flops | bytes accessed | tf_op | source)
XLA Modules:
  0.0 136.4 jit_solution(2369053226362684947)
XLA Ops:
  0.0 134.9 %merge_block.1 = bf16[1024,1280]{1,0:T(8,128)(2,1)S(1)} custom-call(bf16[1024,1280]{1,0:T(8,128)(2,1)} %x_hbm.1, f32[1280]{0:T(1024)} %gain_hbm.1, f32[1280]{0:T(1024)} %shift_hbm.1, bf16[80,1280]{1,0:T(8,128)(2,1)} %merge_hbm.1, bf16[40,1280]{1,0:T(8,128)(2,1)} %outw_hbm.1, s32[3,256]{1,0:T(4,128)} %bitcast.1, s32[256]{0:T(256)} %count_hbm.1), custom_call_target="tpu_custom_call" | custom-call | tf_op jit(solution)/shard_map/merge_block/pallas_call | solution.py:418
  134.9 1.5 %copy.9 = bf16[1024,1280]{1,0:T(8,128)(2,1)} copy(bf16[1024,1280]{1,0:T(8,128)(2,1)S(1)} %merge_block.1) | data formatting | bytes 5242880

commit v7 on v6

--- a/solution.py
+++ b/solution.py
@@ -52,8 +52,8 @@
 def kernel(
     sizes,
     x_hbm, gain_hbm, shift_hbm, merge_hbm, outw_hbm, src_hbm, count_hbm,
-    out_ref,
-    x, params, merge_ref, outw_ref, src_ref, count_ref, stage, send1, recv1, send2, recv2, table, full, merge_w, out_w, acc, act, collect, spread, stats,
+    x, out_w, acc, stats,
+    params, merge_ref, outw_ref, src_ref, count_ref, stage, send1, recv1, send2, recv2, table, full, merge_w, collect, spread,
     load_sem, s1_sem, r1_sem, s2_sem, r2_sem, ws_sem, wr_sem,
 ):
     ys, zs, xs, cores = sizes
@@ -138,6 +138,16 @@
         [tail, jnp.zeros((PIECE - rest, channels), F32)], axis=0
     ).astype(BF16)
 
+    load.wait()
+
+    def total(i, carry):
+        part = x[pl.ds(pl.multiple_of(i * 64, 64), 64), :].astype(F32)
+        return carry + fold_rows(part)
+
+    zeros = jnp.zeros((ROWS, channels), F32)
+    summed = lax.fori_loop(0, rows // 64, total, zeros)
+    average = group_mean(jnp.sum(summed, axis=0, keepdims=True), collect, spread, members)
+
     pl.semaphore_wait(barrier, shards - 1 + xs - 1 + 1)
 
     def beside(dz):
@@ -146,16 +156,6 @@
     pltpu.make_async_copy(stage.at[g], full.at[s, g], wr_sem.at[0]).start()
     for dz in (-2, 2, -1, 1):
         weight_copy(stage.at[g], full.at[s, g], 0, (g, beside(dz))).start()
-
-    load.wait()
-
-    def total(i, carry):
-        part = x[pl.ds(pl.multiple_of(i * 64, 64), 64), :].astype(F32)
-        return carry + fold_rows(part)
-
-    zeros = jnp.zeros((ROWS, channels), F32)
-    summed = lax.fori_loop(0, rows // 64, total, zeros)
-    average = group_mean(jnp.sum(summed, axis=0, keepdims=True), collect, spread, members)
 
     def total_square(i, carry):
         part = x[pl.ds(pl.multiple_of(i * 64, 64), 64), :].astype(F32) - average
@@ -369,6 +369,24 @@
     stats[0:1, :] = moved
     stats[1:2, :] = scale
 
+    for chunk in range(chunks):
+        drain(send1.at[chunk, pl.ds(0, shards - 1)], s1_sem.at[chunk])
+        drain(send2.at[chunk, pl.ds(0, shards - 1)], s2_sem.at[chunk])
+    drain(full.at[pl.ds(0, 4), 0], ws_sem.at[0])
+    drain(full.at[pl.ds(0, 3), 0], ws_sem.at[4])
+    drain(full.at[pl.ds(0, (ys - 1) * zs), 0], ws_sem.at[1])
+    drain(full.at[pl.ds(0, (xs - 1) * shards // pieces)], ws_sem.at[2])
+    drain(full.at[pl.ds(0, xs * shards // pieces)], ws_sem.at[3])
+
+
+def finish(x_ref, out_w, acc, stats, out_hbm, act, result, sem):
+    rows, channels = acc.shape
+    blocks = rows // BLOCK
+    slice_rows = blocks * ROWS
+    tile = width = 256
+    tile_strips = tile // slice_rows
+    tiles, spans = rows // tile, channels // width
+
     def activate(m, n):
         at, columns = slice(m * tile, (m + 1) * tile), slice(n * width, (n + 1) * width)
         value = silu((acc[at, columns] - stats[0:1, columns]) * stats[1:2, columns])
@@ -390,17 +408,12 @@
                     lower = projected[top + slice_rows + block * ROWS : top + slice_rows + (block + 1) * ROWS]
                     start = block * BLOCK + m * (tile_strips * ROWS) + pair * 2 * ROWS
                     to = slice(start, start + 2 * ROWS)
-                    value = x[to, columns].astype(F32) + jnp.concatenate([upper, lower], axis=0)
-                    out_ref[to, columns] = value.astype(BF16)
-
-    for chunk in range(chunks):
-        drain(send1.at[chunk, pl.ds(0, shards - 1)], s1_sem.at[chunk])
-        drain(send2.at[chunk, pl.ds(0, shards - 1)], s2_sem.at[chunk])
-    drain(full.at[pl.ds(0, 4), 0], ws_sem.at[0])
-    drain(full.at[pl.ds(0, 3), 0], ws_sem.at[4])
-    drain(full.at[pl.ds(0, (ys - 1) * zs), 0], ws_sem.at[1])
-    drain(full.at[pl.ds(0, (xs - 1) * shards // pieces)], ws_sem.at[2])
-    drain(full.at[pl.ds(0, xs * shards // pieces)], ws_sem.at[3])
+                    value = x_ref[to, columns].astype(F32) + jnp.concatenate([upper, lower], axis=0)
+                    result[to, columns] = value.astype(BF16)
+        for block in range(blocks):
+            to = pl.ds(block * BLOCK + m * (tile_strips * ROWS), tile_strips * ROWS)
+            pltpu.make_async_copy(result.at[to], out_hbm.at[to], sem).start()
+    pltpu.make_async_copy(result, out_hbm, sem).wait()
 
 
 def solution(mesh):
@@ -415,13 +428,19 @@
         hbm = pl.BlockSpec(memory_space=pltpu.HBM)
         slices = pltpu.VMEM((chunks, shards, slice_rows, LANES), BF16)
         dma = pltpu.SemaphoreType.DMA
-        return pl.pallas_call(
+        vmem = pl.BlockSpec(memory_space=pltpu.VMEM)
+        whole = pltpu.VMEM(features.shape, BF16)
+        handed = pl.pallas_call(
             functools.partial(kernel, sizes),
-            out_shape=pltpu.VMEM(features.shape, features.dtype),
+            out_shape=[
+                whole,
+                pltpu.VMEM((channels, channels), BF16),
+                pltpu.VMEM((rows, channels), F32),
+                pltpu.VMEM((ROWS, channels), F32),
+            ],
             in_specs=[hbm] * 7,
-            out_specs=pl.BlockSpec(memory_space=pltpu.VMEM),
+            out_specs=[vmem] * 4,
             scratch_shapes=[
-                pltpu.VMEM((rows, channels), BF16),
                 pltpu.VMEM((ROWS, channels), F32),
                 pltpu.VMEM(merge_weight.shape, BF16),
                 pltpu.VMEM(out_weight.shape, BF16),
@@ -432,18 +451,14 @@
                 pltpu.VMEM((corr_src.shape[0], ROWS, LANES), F32),
                 pltpu.VMEM((shards, groups, PIECE, channels), BF16),
                 pltpu.VMEM((2 * channels, channels), BF16),
-                pltpu.VMEM((channels, channels), BF16),
-                pltpu.VMEM((rows, channels), F32),
-                pltpu.VMEM((rows, channels), BF16),
                 pltpu.VMEM((channels, LANES), BF16),
                 pltpu.VMEM((LANES, channels), BF16),
-                pltpu.VMEM((ROWS, channels), F32),
                 dma((7,)),
                 dma((chunks,)), dma((chunks,)), dma((chunks,)), dma((chunks,)),
                 dma((5,)), dma((5,)),
             ],
             compiler_params=pltpu.CompilerParams(
-                collective_id=0, has_side_effects=True, vmem_limit_bytes=44 * 1024 * 1024
+                collective_id=0, has_side_effects=True, vmem_limit_bytes=42 * 1024 * 1024
             ),
             name="merge_block",
         )(
@@ -454,6 +469,15 @@
                 )
             )
         )
+        return pl.pallas_call(
+            finish,
+            out_shape=jax.ShapeDtypeStruct(features.shape, features.dtype),
+            in_specs=[vmem] * 4,
+            out_specs=pl.BlockSpec(memory_space=pl.ANY),
+            scratch_shapes=[whole, whole, dma],
+            compiler_params=pltpu.CompilerParams(vmem_limit_bytes=20 * 1024 * 1024),
+            name="finish_block",
+        )(*handed)
 
     placed = (
         P(("grp", "shard"), None),

time: 136 us -> 135 us (level)
  local copies, waits for them, and re-layouts: 1.49 us -> 0 us
    unnamed x1 -> x0, local copies, waits for them, and re-layouts: 1.49 us -> none
    pallas_call x1 -> x2, Pallas kernels: 135 us -> 135 us  [the longest x1 131 us: per_device(): pl.pallas_call(functools.partial(kernel, sizes), out_shape=[whole, pltpu....]
where the time goes in v7:
time: 135 us
  Pallas kernels  135 us (100%)
    pallas_call x1, Pallas kernels, per_device(): pl.pallas_call(functools.partial(kernel, sizes), out_shape=[whole, pltpu....  131 us
    pallas_call x1, Pallas kernels, per_device(): pl.pallas_call(finish, out_shape=jax.ShapeDtypeStruct(features.shape, fea...  4.53 us

profile of v7, /device:TPU:1, one launch (start us, length us, event | category | flops | bytes accessed | tf_op | source)
XLA Modules:
  0.0 135.1 jit_solution(17935766219239859399)
XLA Ops:
  0.0 130.6 %merge_block.1 = (bf16[1024,1280]{1,0:T(8,128)(2,1)S(1)}, bf16[1280,1280]{1,0:T(8,128)(2,1)S(1)}, f32[1024,1280]{1,0:T(8,128)S(1)}, f32[8,1280]{1,0:T(8,128)S(1)}) custom-call(bf16[1024,1280]{1,0:T(8,128)(2,1)} %x_hbm.1, f32[1280]{0:T(1024)} %gain_hbm.1, f32[1280]{0:T(1024)} %shift_hbm.1, bf16[80,1280]{1,0:T(8,128)(2,1)} %merge_hbm.1, ...), custom_call_target="tpu_custom_call" | custom-call | tf_op jit(solution)/shard_map/merge_block/pallas_call | solution.py:433
  130.6 4.5 %finish_block.1 = bf16[1024,1280]{1,0:T(8,128)(2,1)} custom-call(bf16[1024,1280]{1,0:T(8,128)(2,1)S(1)} %get-tuple-element.9.x_ref, bf16[1280,1280]{1,0:T(8,128)(2,1)S(1)} %get-tuple-element.10.out_w, f32[1024,1280]{1,0:T(8,128)S(1)} %get-tuple-element.11.acc, f32[8,1280]{1,0:T(8,128)S(1)} %get-tuple-element.12.stats), custom_call_target="tpu_custom_call" | custom-call | tf_op jit(solution)/shard_map/finish_block/pallas_call | solution.py:472

commit v8 on v7

--- a/solution.py
+++ b/solution.py
@@ -396,6 +396,7 @@
         activate(0, n)
     for m in range(tiles):
         at = slice(m * tile, (m + 1) * tile)
+        sent = 0
         for n in range(spans):
             columns = slice(n * width, (n + 1) * width)
             projected = jnp.dot(act[at, :], out_w[:, columns], preferred_element_type=F32)
@@ -409,10 +410,15 @@
                     start = block * BLOCK + m * (tile_strips * ROWS) + pair * 2 * ROWS
                     to = slice(start, start + 2 * ROWS)
                     value = x_ref[to, columns].astype(F32) + jnp.concatenate([upper, lower], axis=0)
-                    result[to, columns] = value.astype(BF16)
-        for block in range(blocks):
-            to = pl.ds(block * BLOCK + m * (tile_strips * ROWS), tile_strips * ROWS)
-            pltpu.make_async_copy(result.at[to], out_hbm.at[to], sem).start()
+                    inside = slice(start - block * BLOCK, start - block * BLOCK + 2 * ROWS)
+                    result[block, inside, columns] = value.astype(BF16)
+            if n in (2, spans - 1):
+                rows_of = pl.ds(m * tile_strips * ROWS, tile_strips * ROWS)
+                columns = pl.ds(sent * width, (n + 1 - sent) * width)
+                pltpu.make_async_copy(
+                    result.at[:, rows_of, columns], out_hbm.at[:, rows_of, columns], sem
+                ).start()
+                sent = n + 1
     pltpu.make_async_copy(result, out_hbm, sem).wait()
 
 
@@ -469,15 +475,16 @@
                 )
             )
         )
+        blocked = (rows // BLOCK, BLOCK, channels)
         return pl.pallas_call(
             finish,
-            out_shape=jax.ShapeDtypeStruct(features.shape, features.dtype),
+            out_shape=jax.ShapeDtypeStruct(blocked, features.dtype),
             in_specs=[vmem] * 4,
             out_specs=pl.BlockSpec(memory_space=pl.ANY),
-            scratch_shapes=[whole, whole, dma],
+            scratch_shapes=[whole, pltpu.VMEM(blocked, BF16), dma],
             compiler_params=pltpu.CompilerParams(vmem_limit_bytes=20 * 1024 * 1024),
             name="finish_block",
-        )(*handed)
+        )(*handed).reshape(features.shape)
 
     placed = (
         P(("grp", "shard"), None),

time: 135 us -> 137 us (1.015)
  Pallas kernels: 135 us -> 137 us
    pallas_call x1, Pallas kernels: 4.53 us -> 6.36 us  [per_device(): pl.pallas_call(finish, out_shape=jax.ShapeDtypeStruct(blocked, features.d...]
where the time goes in v8:
time: 137 us
  Pallas kernels  137 us (100%)
    pallas_call x1, Pallas kernels, per_device(): pl.pallas_call(functools.partial(kernel, sizes), out_shape=[whole, pltpu....  131 us
    pallas_call x1, Pallas kernels, per_device(): pl.pallas_call(finish, out_shape=jax.ShapeDtypeStruct(blocked, features.d...  6.36 us

profile of v8, /device:TPU:1, one launch (start us, length us, event | category | flops | bytes accessed | tf_op | source)
XLA Modules:
  0.0 137.0 jit_solution(12977709333451583633)
XLA Ops:
  0.0 130.6 %merge_block.1 = (bf16[1024,1280]{1,0:T(8,128)(2,1)S(1)}, bf16[1280,1280]{1,0:T(8,128)(2,1)S(1)}, f32[1024,1280]{1,0:T(8,128)S(1)}, f32[8,1280]{1,0:T(8,128)S(1)}) custom-call(bf16[1024,1280]{1,0:T(8,128)(2,1)} %x_hbm.1, f32[1280]{0:T(1024)} %gain_hbm.1, f32[1280]{0:T(1024)} %shift_hbm.1, bf16[80,1280]{1,0:T(8,128)(2,1)} %merge_hbm.1, ...), custom_call_target="tpu_custom_call" | custom-call | tf_op jit(solution)/shard_map/merge_block/pallas_call | solution.py:439
  130.6 6.4 %finish_block.1 = bf16[8,128,1280]{2,1,0:T(8,128)(2,1)} custom-call(bf16[1024,1280]{1,0:T(8,128)(2,1)S(1)} %get-tuple-element.9.x_ref, bf16[1280,1280]{1,0:T(8,128)(2,1)S(1)} %get-tuple-element.10.out_w, f32[1024,1280]{1,0:T(8,128)S(1)} %get-tuple-element.11.acc, f32[8,1280]{1,0:T(8,128)S(1)} %get-tuple-element.12.stats), custom_call_target="tpu_custom_call" | custom-call | tf_op jit(solution)/shard_map/finish_block/pallas_call | solution.py:479
